TPU v7x, 256 devices: a whole 4x4x8 slice. The times are simulated.
256 devices in a mesh: img: 16 (over z, y_hi), txt: 16 (over y_lo, x, core).
Axes of the slice: x: 4, y: 4 (y_hi: 2, y_lo: 2; y = y_hi * 2 + y_lo), z: 8, core: 2. Of those that a mesh axis runs over, the one named last changes fastest.
Arguments:
- image_emb: bfloat16 [16384, 1152], P(('img', 'txt')), may hold values from -6 to 6
- text_emb: bfloat16 [16384, 1152], P(('txt', 'img')), may hold values from -6 to 6
- positive: int32 [16384], P('img'), may hold values from 0 to 16383, each once
- loss_scale: float32 [], replicated, may hold values from 256 to 1024
Outputs:
- grad_image: bfloat16 [16384, 1152], P(('img', 'txt'))
- grad_text: bfloat16 [16384, 1152], P(('txt', 'img'))
Inputs may be any that keep to these rules, and one draw needn't show every extreme that they name: `positive`: every text is the pair of exactly one image.
All inputs are finite; a program needn't handle non-finite values.
Results may differ from a plain program's by a relative error of at most 0.0088.
Values may be sent and summed in bfloat16 or wider, within the bound.
No kernel may reach another device: no remote copies, remote signals or barrier semaphores. Data moves between devices by JAX's collectives and lax.ppermute only.
A program may use at most 64 MiB of HBM per device.

v0:
```python
import functools

import jax
import jax.numpy as jnp
import numpy as np
from jax import lax
from jax.experimental import pallas as pl
from jax.experimental.pallas import tpu as pltpu
from jax.sharding import PartitionSpec as P

temper = 32.0
offset = -2.0
epsilon = 1e-06
F32 = jnp.float32
BF16 = jnp.bfloat16
AXES = ("img", "txt")
NX, NY, NZ = 4, 4, 8
VMEM_LIMIT = 16 * 1024 * 1024


def line(z, y, x, c):
    return ((z * 2 + y // 2) * 2 + y % 2) * (NX * 2) + x * 2 + c


def make_perm(move):
    pairs = []
    for z in range(NZ):
        for y in range(NY):
            for x in range(NX):
                for c in range(2):
                    tz, ty, tx, tc = move(z, y, x, c, 1 - 2 * c)
                    pairs.append((line(z, y, x, c), line(tz % NZ, ty % NY, tx % NX, tc)))
    return pairs


CORE = make_perm(lambda z, y, x, c, s: (z, y, x, 1 - c))
Z_ONE = make_perm(lambda z, y, x, c, s: (z + s, y, x, c))
Z_TWO = make_perm(lambda z, y, x, c, s: (z + 2 * s, y, x, c))


def shift_perm(first, by):
    return make_perm(
        lambda z, y, x, c, s: (z, y, x + by, c) if (c == 0) == first else (z, y + by, x, c)
    )


A_ON, A_BACK, A_TWO = (shift_perm(True, by) for by in (1, -1, 2))
B_ON, B_BACK, B_TWO = (shift_perm(False, by) for by in (1, -1, 2))
Y_TWO = make_perm(lambda z, y, x, c, s: (z, y + 2, x, c))


def send(v, perm):
    return lax.ppermute(v, AXES, perm)


def wide_inv(raw):
    wide = raw.astype(F32)
    return wide, lax.rsqrt(jnp.sum(wide * wide, axis=1, keepdims=True) + epsilon)


def project(raw, d):
    wide, inv = wide_inv(raw)
    unit = wide * inv
    dots = jnp.sum(unit * d, axis=1, keepdims=True)
    return ((d - unit * dots) * inv).astype(BF16)


def join_kernel(*refs):
    row = 0
    for p in refs[:-1]:
        n = p.shape[0]
        refs[-1][row : row + n, :] = p[...]
        row += n


def norm_kernel(*refs):
    pieces, out = refs[:-1], refs[-1]
    row = 0
    for p in pieces:
        n = p.shape[0]
        wide, inv = wide_inv(p[...])
        out[row : row + n, :] = (wide * inv).astype(BF16)
        row += n


def setup_kernel(tab_ref, scale_ref, own_ref, across_ref, pos_ref, ids_ref, weight_ref):
    core = tab_ref[48]
    for k in range(4):
        parts = []
        for j in range(4 * k, 4 * k + 4):
            at = pl.ds(tab_ref[16 + j], 1)
            both = jnp.where(tab_ref[32 + j] == 1, own_ref[at, :], across_ref[at, :])
            parts.append(jnp.where(core == 0, both[:, :64], both[:, 64:]))
        pos_ref[k : k + 1, :] = jnp.concatenate(parts, axis=1)
    row = lax.broadcasted_iota(jnp.int32, (64, 128), 0)
    for b in range(16):
        ids_ref[b * 64 : b * 64 + 64, :] = row + tab_ref[b]
    weight_ref[...] = jnp.full(weight_ref.shape, scale_ref[0], F32)


def tile_kernel(quarter, weight_ref, pos_ref, ids_ref, xh_ref, yh_ref, g_ref):
    texts, images = g_ref.shape
    weight = weight_ref[0:1, :]
    pos = pos_ref[quarter : quarter + 1, :]
    for m in range(0, texts, 512):
        rows = slice(m, m + 512)
        logits = (
            temper
            * lax.dot_general(
                yh_ref[rows, :], xh_ref[...], (((1,), (1,)), ((), ())), preferred_element_type=F32
            )
            + offset
        )
        half = jax.nn.sigmoid(logits)
        for n in range(0, images, 128):
            cols = slice(n, n + 128)
            same = (pos[:, cols] == ids_ref[rows, :]).astype(F32)
            g_ref[rows, cols] = (weight * (half[:, cols] - same)).astype(BF16)


def image_kernel(raw_ref, yh_ref, g_ref, out_ref, d_ref):
    width = yh_ref.shape[1]
    for n in range(0, width, 384):
        d_ref[:, n : n + 384] = lax.dot_general(
            g_ref[...], yh_ref[:, n : n + 384], (((0,), (0,)), ((), ())), preferred_element_type=F32
        )
    out_ref[...] = project(raw_ref[...], d_ref[...])


def text_kernel(first, *refs):
    gs, xs, pieces = refs[:4], refs[4:8], refs[8:-2]
    out_ref, d_ref = refs[-2:]
    rows, width = out_ref.shape
    for n in range(0, width, 384):
        total = None
        for g, x in zip(gs, xs):
            part = jnp.dot(
                g[first : first + rows, :], x[:, n : n + 384], preferred_element_type=F32
            )
            total = part if total is None else total + part
        d_ref[:, n : n + 384] = total
    row = 0
    for p in pieces:
        n = p.shape[0]
        out_ref[row : row + n, :] = project(p[...], d_ref[row : row + n, :])
        row += n


VM = pl.BlockSpec(memory_space=pltpu.VMEM)
SM = pl.BlockSpec(memory_space=pltpu.SMEM)
PARAMS = pltpu.CompilerParams(vmem_limit_bytes=VMEM_LIMIT)


def sds(shape, dtype):
    return jax.ShapeDtypeStruct(shape, dtype)


WEIGHT = 0.1


def fast(*arrays):
    return [pltpu.with_memory_space_constraint(a, pltpu.VMEM) for a in arrays]


def cost(us):
    return pl.CostEstimate(flops=int(us * WEIGHT * 1.15e9), bytes_accessed=1, transcendentals=0)


def join(*pieces):
    rows = sum(p.shape[0] for p in pieces)
    width = pieces[0].shape[1]
    return pl.pallas_call(
        join_kernel,
        out_shape=sds((rows, width), BF16),
        in_specs=[VM] * len(pieces),
        out_specs=VM,
        compiler_params=PARAMS,
        cost_estimate=cost(0.3),
        name="join",
    )(*fast(*pieces))


def copy_kernel(*refs):
    half = len(refs) // 2
    for src, dst in zip(refs[:half], refs[half:]):
        dst[...] = src[...]


def fetch(*arrays, us=0.3):
    return pl.pallas_call(
        copy_kernel,
        out_shape=tuple(sds(a.shape, a.dtype) for a in arrays),
        in_specs=[VM] * len(arrays),
        out_specs=tuple([VM] * len(arrays)),
        compiler_params=PARAMS,
        cost_estimate=cost(us),
        name="fetch",
    )(*fast(*arrays))


def head_kernel(src, dst):
    dst[...] = src[: dst.shape[0], :]


def head(array, rows):
    return pl.pallas_call(
        head_kernel,
        out_shape=pltpu.VMEM((rows, array.shape[1]), array.dtype),
        in_specs=[VM],
        out_specs=VM,
        compiler_params=PARAMS,
        cost_estimate=cost(0.1),
        name="head",
    )(*fast(array))


def normalize(*pieces, us=0.8):
    rows = sum(p.shape[0] for p in pieces)
    width = pieces[0].shape[1]
    return pl.pallas_call(
        norm_kernel,
        out_shape=sds((rows, width), BF16),
        in_specs=[VM] * len(pieces),
        out_specs=VM,
        compiler_params=PARAMS,
        cost_estimate=cost(us),
        name="normalize",
    )(*fast(*pieces))


def setup(tab, scale, own, across):
    return pl.pallas_call(
        setup_kernel,
        out_shape=(sds((4, 256), jnp.int32), sds((1024, 128), jnp.int32), sds((8, 128), F32)),
        in_specs=[SM, SM, VM, VM],
        out_specs=(VM, VM, VM),
        compiler_params=PARAMS,
        cost_estimate=cost(1),
        name="setup",
    )(tab, scale, own, across)


def tile(quarter, weight, pos, ids, xh, yh):
    return pl.pallas_call(
        functools.partial(tile_kernel, quarter),
        out_shape=sds((yh.shape[0], xh.shape[0]), BF16),
        in_specs=[VM] * 5,
        out_specs=VM,
        compiler_params=PARAMS,
        cost_estimate=cost(1.3),
        name="tile",
    )(*fast(weight, pos, ids, xh, yh))


def image_sum(raw, yh, g):
    return pl.pallas_call(
        image_kernel,
        out_shape=sds(raw.shape, BF16),
        in_specs=[VM] * 3,
        out_specs=VM,
        scratch_shapes=[pltpu.VMEM(raw.shape, F32)],
        compiler_params=PARAMS,
        cost_estimate=cost(1.6),
        name="image_sum",
    )(*fast(raw, yh, g))


def text_sum(first, gs, xs, pieces, name):
    rows = sum(p.shape[0] for p in pieces)
    width = pieces[0].shape[1]
    return pl.pallas_call(
        functools.partial(text_kernel, first),
        out_shape=sds((rows, width), BF16),
        in_specs=[VM] * (8 + len(pieces)),
        out_specs=VM,
        scratch_shapes=[pltpu.VMEM((rows, width), F32)],
        compiler_params=PARAMS,
        cost_estimate=cost(rows / 230),
        name=name,
    )(*fast(*gs, *xs, *pieces))


def add(*terms):
    total = terms[0].astype(F32)
    for t in terms[1:]:
        total = total + t.astype(F32)
    return total


def local(image_emb, text_emb, positive, loss_scale):
    i, t = lax.axis_index("img"), lax.axis_index("txt")
    z, yh = i // 2, i % 2
    yl, x, c = t // 8, (t // 2) % 4, t % 2
    y = yh * 2 + yl
    s = 1 - 2 * c
    d = 1 - c

    other = send(text_emb, CORE)
    images, text_emb = fetch(image_emb, text_emb)
    chip = join(text_emb, other)
    one = send(chip, Z_ONE)
    two = send(chip, Z_TWO)
    def text_base(zz, cc):
        return ((((yl * 4 + x) * 2 + cc) * 8 + zz % 8) * 2 + yh) * 64

    at = [(z - 3 * s, c), (z - 3 * s, d), (z + 4, c)]
    at += [(z + 3 * s, d), (z + 3 * s, c), (z + 4, d)]
    at += [(z - s, c), (z - s, d), (z - 2 * s, c), (z - 2 * s, d), (z, d)]
    at += [(z + s, d), (z + s, c), (z + 2 * s, d), (z + 2 * s, c), (z, c)]
    table = [text_base(*p) for p in at]
    rows, mine = [], []
    for b in (0, -1, 1, 2):
        for a in (0, -1, 1, 2):
            yy = (y + jnp.where(c == 0, b, a)) % 4
            xx = (x + jnp.where(c == 0, a, b)) % 4
            rows.append(yy % 2 * 4 + xx)
            mine.append((yy // 2 == yh).astype(jnp.int32))
    tab = jnp.stack([v.astype(jnp.int32) for v in table + rows + mine + [c]])
    scale = (loss_scale * (temper / 16384.0)).reshape(1)
    own_pairs = positive.reshape(8, 128)
    own_pairs, two = lax.optimization_barrier((own_pairs, two))
    across_pairs = send(own_pairs, Y_TWO)
    pos, ids, weight = setup(tab, scale, own_pairs, across_pairs)

    three = send(two, Z_ONE)
    four = send(head(two, 64), Z_TWO)
    far_give = [three, four]
    far_keep = [send(three, CORE), send(four, CORE)]
    near_give = [one, two, other]
    near_keep = [send(one, CORE), send(two, CORE), text_emb]

    row = join(images, send(image_emb, A_ON), send(image_emb, A_BACK), send(image_emb, A_TWO))
    quarters = [row, send(row, B_ON), send(row, B_BACK), send(row, B_TWO)]
    xs = [normalize(quarters[0], us=0.3)] + [normalize(q, us=10) for q in quarters[1:]]

    yh_all = normalize(*far_give, *far_keep, *near_give, *near_keep)
    gs = [tile(k, weight, pos, ids, xs[k], yh_all) for k in range(4)]
    d_give = text_sum(0, gs, xs, far_give, "far_give")
    swapped = send(d_give, CORE)
    d_keep = text_sum(192, gs, xs, far_keep, "far_keep")
    far_sum = add(d_keep, swapped).astype(BF16)
    relay = send(far_sum, Z_TWO)

    far_sum, *gs = lax.optimization_barrier((far_sum, *gs))
    es = [image_sum(quarters[k], yh_all, gs[k]) for k in range(4)]
    back = [send(es[1], B_BACK), send(es[2], B_ON), send(es[3], B_TWO)]

    _, *gs = lax.optimization_barrier((es[3], *gs))
    d_give = text_sum(384, gs, xs, near_give, "near_give")
    swapped = send(d_give, CORE)
    d_keep = text_sum(704, gs, xs, near_keep, "near_keep")
    near_sum = add(d_keep, swapped)
    (relay,) = fetch(relay, us=40)
    half = add(near_sum[0:192], relay).astype(BF16)
    own_sum, half = lax.optimization_barrier((es[0], half))
    row_sum = add(own_sum, *back)
    row_half = row_sum.astype(BF16)
    home = [send(row_half[64:128], A_BACK), send(row_half[128:192], A_ON), send(row_half[192:256], A_TWO)]
    grad_image = add(row_sum[:64], *home).astype(BF16)

    w1 = send(half[0:128], Z_ONE)
    w2 = send(jnp.concatenate([half[128:192], near_sum[192:256].astype(BF16)], axis=0), Z_TWO)
    w1, w2 = fetch(w1, w2, us=40)
    to_other = add(w1[:64], w2[:64]).astype(BF16)
    last = send(to_other, CORE)
    grad_text = add(near_sum[256:320], w1[64:], w2[64:], last).astype(BF16)
    return grad_image, grad_text


def solution(mesh):
    in_specs = (P(("img", "txt"), None), P(("txt", "img"), None), P("img"), P())
    out_specs = (P(("img", "txt"), None), P(("txt", "img"), None))
    return jax.shard_map(local, mesh=mesh, in_specs=in_specs, out_specs=out_specs, check_vma=False)
```

profile of v0, /device:TPU:1, one launch (start us, length us, event | category | flops | bytes accessed | tf_op | source)
XLA Modules:
  0.0 87.2 jit_solution(8509493379454671480)
XLA Ops:
  0.6 3.3 %collective-permute-start.3 = (bf16[64,1152]{1,0:T(8,128)(2,1)}, bf16[64,1152]{1,0:T(8,128)(2,1)S(1)}, u32[]{:S(2)}, u32[]{:S(2)}) collective-permute-start(bf16[64,1152]{1,0:T(8,128)(2,1)} %refs_1_.1), channel_id=1, source_target_pairs={{0,1},{1,0},{2,3},{3,2},{4,5},{5,4},{6,7},{7,6},{8,9},{9,8},{10,11... | collective-permute-start | bytes 442376 | tf_op jit(solution)/shard_map/ppermute | solution.py:53
  4.0 2.2 %collective-permute-start.2 = (bf16[64,1152]{1,0:T(8,128)(2,1)}, bf16[64,1152]{1,0:T(8,128)(2,1)S(1)}, u32[]{:S(2)}, u32[]{:S(2)}) collective-permute-start(bf16[64,1152]{1,0:T(8,128)(2,1)} %refs_0_.1), channel_id=1, source_target_pairs={{0,4},{1,17},{2,6},{3,19},{4,0},{5,21},{6,2},{7,23},{8,12},{9,25},... | collective-permute-start | bytes 442376 | tf_op jit(solution)/shard_map/ppermute | solution.py:53
  9.1 6.1 %collective-permute-start.4 = (bf16[128,1152]{1,0:T(8,128)(2,1)S(1)}, bf16[128,1152]{1,0:T(8,128)(2,1)S(1)}, u32[]{:S(2)}, u32[]{:S(2)}) collective-permute-start(bf16[128,1152]{1,0:T(8,128)(2,1)S(1)} %join.3), channel_id=1, source_target_pairs={{0,64},{1,193},{2,66},{3,195},{4,68},{5,197},{6,70},{7,199},{8,72}... | collective-permute-start | bytes 884744 | tf_op jit(solution)/shard_map/ppermute | solution.py:53
  15.3 2.8 %collective-permute-start.15 = (bf16[256,1152]{1,0:T(8,128)(2,1)S(1)}, bf16[256,1152]{1,0:T(8,128)(2,1)S(1)}, u32[]{:S(2)}, u32[]{:S(2)}) collective-permute-start(bf16[256,1152]{1,0:T(8,128)(2,1)S(1)} %join.2.refs_0_.raw_ref), channel_id=1, source_target_pairs={{0,16},{1,5},{2,18},{3,7},{4,20},{5,1},{6,22},{7,3},{8,24},{9,13},... | collective-permute-start | bytes 1769480 | tf_op jit(solution)/shard_map/ppermute | solution.py:53
  20.6 1.5 %collective-permute-done.4.src.refs_5_.refs_9_ = bf16[128,1152]{1,0:T(8,128)(2,1)S(1)} collective-permute-done((bf16[128,1152]{1,0:T(8,128)(2,1)S(1)}, bf16[128,1152]{1,0:T(8,128)(2,1)S(1)}, u32[]{:S(2)}, u32[]{:S(2)}) %collective-permute-start.4) | collective-permute-done | bytes 294944 | tf_op jit(solution)/shard_map/ppermute | solution.py:53
  22.0 2.4 %collective-permute-start.5 = (bf16[128,1152]{1,0:T(8,128)(2,1)S(1)}, bf16[128,1152]{1,0:T(8,128)(2,1)S(1)}, u32[]{:S(2)}, u32[]{:S(2)}) collective-permute-start(bf16[128,1152]{1,0:T(8,128)(2,1)S(1)} %collective-permute-done.4.src.refs_5_.refs_9_), channel_id=1, source_target_pairs={{0,32},{1,225},{2,34},{3,227},{4,36},{5,229},{6,38},{7,231},{8,40}... | collective-permute-start | bytes 884744 | tf_op jit(solution)/shard_map/ppermute | solution.py:53
  27.0 2.2 %collective-permute-done.12.across_ref = s32[8,128]{1,0:T(8,128)S(1)} collective-permute-done((s32[8,128]{1,0:T(8,128)S(1)}, s32[8,128]{1,0:T(8,128)S(1)}, u32[]{:S(2)}, u32[]{:S(2)}) %collective-permute-start.12) | collective-permute-done | bytes 4128 | tf_op jit(solution)/shard_map/ppermute | solution.py:53
  29.3 2.7 %collective-permute-start.6 = (bf16[64,1152]{1,0:T(8,128)(2,1)}, bf16[64,1152]{1,0:T(8,128)(2,1)}, u32[]{:S(2)}, u32[]{:S(2)}) collective-permute-start(bf16[64,1152]{1,0:T(8,128)(2,1)} %head.1), channel_id=1, source_target_pairs={{0,64},{1,193},{2,66},{3,195},{4,68},{5,197},{6,70},{7,199},{8,72}... | collective-permute-start | bytes 442376 | tf_op jit(solution)/shard_map/ppermute | solution.py:53
  33.8 1.7 %collective-permute-done.6.refs_1_.refs_9_ = bf16[64,1152]{1,0:T(8,128)(2,1)} collective-permute-done((bf16[64,1152]{1,0:T(8,128)(2,1)}, bf16[64,1152]{1,0:T(8,128)(2,1)}, u32[]{:S(2)}, u32[]{:S(2)}) %collective-permute-start.6) | collective-permute-done | bytes 147488 | tf_op jit(solution)/shard_map/ppermute | solution.py:53
  35.6 4.1 %collective-permute-start.11 = (bf16[128,1152]{1,0:T(8,128)(2,1)S(1)}, bf16[128,1152]{1,0:T(8,128)(2,1)S(1)}, u32[]{:S(2)}, u32[]{:S(2)}) collective-permute-start(bf16[128,1152]{1,0:T(8,128)(2,1)S(1)} %collective-permute-done.4.src.refs_5_.refs_9_), channel_id=1, source_target_pairs={{0,1},{1,0},{2,3},{3,2},{4,5},{5,4},{6,7},{7,6},{8,9},{9,8},{10,11... | collective-permute-start | bytes 884744 | tf_op jit(solution)/shard_map/ppermute | solution.py:53
  42.2 1.6 %normalize.5.yh_ref = bf16[1024,1152]{1,0:T(8,128)(2,1)S(1)} custom-call(bf16[128,1152]{1,0:T(8,128)(2,1)S(1)} %collective-permute-done.5.refs_0_.refs_8_, bf16[64,1152]{1,0:T(8,128)(2,1)} %collective-permute-done.6.refs_1_.refs_9_, bf16[128,1152]{1,0:T(8,128)(2,1)S(1)} %collective-permute-done.7.refs_2_.refs_8_, ...), custom_call_target="tpu_custom_call" | custom-call | flops 92000000 | bytes 1 | tf_op jit(solution)/shard_map/normalize/pallas_call | solution.py:220
  48.1 1.8 %far_give.1 = bf16[192,1152]{1,0:T(8,128)(2,1)S(1)} custom-call(bf16[1024,256]{1,0:T(8,128)(2,1)S(1)} %tile.4.refs_0_.g_ref, bf16[1024,256]{1,0:T(8,128)(2,1)S(1)} %tile.5.refs_1_.g_ref, bf16[1024,256]{1,0:T(8,128)(2,1)S(1)} %tile.6.refs_2_.g_ref, bf16[1024,256]{1,0:T(8,128)(2,1)S(1)} %tile.7.refs_3_.g_ref, bf16[256,1152]{1,0:T(8,128)(2,1)S(1)} %normalize.6.xh_ref.refs_4_, ...), custom_call_target="tpu_custom_call" | custom-call | flops 96000000 | bytes 1 | tf_op jit(solution)/shard_map/far_give/pallas_call | solution.py:271
  51.9 2.7 %collective-permute-start.18 = (bf16[192,1152]{1,0:T(8,128)(2,1)S(1)}, bf16[192,1152]{1,0:T(8,128)(2,1)S(1)}, u32[]{:S(2)}, u32[]{:S(2)}) collective-permute-start(bf16[192,1152]{1,0:T(8,128)(2,1)S(1)} %add_convert_fusion), channel_id=1, source_target_pairs={{0,64},{1,193},{2,66},{3,195},{4,68},{5,197},{6,70},{7,199},{8,72}... | collective-permute-start | bytes 1327112 | tf_op jit(solution)/shard_map/ppermute | solution.py:53
  55.8 1.4 %near_give.1 = bf16[320,1152]{1,0:T(8,128)(2,1)S(1)} custom-call(bf16[1024,256]{1,0:T(8,128)(2,1)S(1)} %tile.4.refs_0_.g_ref, bf16[1024,256]{1,0:T(8,128)(2,1)S(1)} %tile.5.refs_1_.g_ref, bf16[1024,256]{1,0:T(8,128)(2,1)S(1)} %tile.6.refs_2_.g_ref, bf16[1024,256]{1,0:T(8,128)(2,1)S(1)} %tile.7.refs_3_.g_ref, bf16[256,1152]{1,0:T(8,128)(2,1)S(1)} %normalize.6.xh_ref.refs_4_, ...), custom_call_target="tpu_custom_call" | custom-call | flops 160000000 | bytes 1 | tf_op jit(solution)/shard_map/near_give/pallas_call | solution.py:271
  57.3 2.2 %collective-permute-start.21 = (bf16[256,1152]{1,0:T(8,128)(2,1)S(1)}, bf16[256,1152]{1,0:T(8,128)(2,1)S(1)}, u32[]{:S(2)}, u32[]{:S(2)}) collective-permute-start(bf16[256,1152]{1,0:T(8,128)(2,1)S(1)} %image_sum.5), channel_id=1, source_target_pairs={{0,16},{1,5},{2,18},{3,7},{4,20},{5,1},{6,22},{7,3},{8,24},{9,13},... | collective-permute-start | bytes 1769480 | tf_op jit(solution)/shard_map/ppermute | solution.py:53
  63.0 2.0 %collective-permute-start.19 = (bf16[256,1152]{1,0:T(8,128)(2,1)S(1)}, bf16[256,1152]{1,0:T(8,128)(2,1)S(1)}, u32[]{:S(2)}, u32[]{:S(2)}) collective-permute-start(bf16[256,1152]{1,0:T(8,128)(2,1)S(1)} %image_sum.6), channel_id=1, source_target_pairs={{0,24},{1,7},{2,26},{3,1},{4,28},{5,3},{6,30},{7,5},{8,0},{9,15},{... | collective-permute-start | bytes 1769480 | tf_op jit(solution)/shard_map/ppermute | solution.py:53
  65.0 1.4 %near_keep.1 = bf16[320,1152]{1,0:T(8,128)(2,1)S(1)} custom-call(bf16[1024,256]{1,0:T(8,128)(2,1)S(1)} %tile.4.refs_0_.g_ref, bf16[1024,256]{1,0:T(8,128)(2,1)S(1)} %tile.5.refs_1_.g_ref, bf16[1024,256]{1,0:T(8,128)(2,1)S(1)} %tile.6.refs_2_.g_ref, bf16[1024,256]{1,0:T(8,128)(2,1)S(1)} %tile.7.refs_3_.g_ref, bf16[256,1152]{1,0:T(8,128)(2,1)S(1)} %normalize.6.xh_ref.refs_4_, ...), custom_call_target="tpu_custom_call" | custom-call | flops 160000000 | bytes 1 | tf_op jit(solution)/shard_map/near_keep/pallas_call | solution.py:271
  66.4 1.2 %image_sum.4 = bf16[256,1152]{1,0:T(8,128)(2,1)S(1)} custom-call(bf16[256,1152]{1,0:T(8,128)(2,1)S(1)} %join.2.refs_0_.raw_ref, bf16[1024,1152]{1,0:T(8,128)(2,1)S(1)} %normalize.5.yh_ref, bf16[1024,256]{1,0:T(8,128)(2,1)S(1)} %tile.4.refs_0_.g_ref), custom_call_target="tpu_custom_call" | custom-call | flops 184000000 | bytes 1 | tf_op jit(solution)/shard_map/image_sum/pallas_call | solution.py:256
  68.0 3.8 %collective-permute-start.26 = (bf16[128,1152]{1,0:T(8,128)(2,1)S(1)}, bf16[128,1152]{1,0:T(8,128)(2,1)S(1)}, u32[]{:S(2)}, u32[]{:S(2)}) collective-permute-start(bf16[128,1152]{1,0:T(8,128)(2,1)S(1)} %pad_maximum_fusion), channel_id=1, source_target_pairs={{0,64},{1,193},{2,66},{3,195},{4,68},{5,197},{6,70},{7,199},{8,72}... | collective-permute-start | bytes 884744 | tf_op jit(solution)/shard_map/ppermute | solution.py:53
  72.0 2.2 %collective-permute-done.20 = bf16[256,1152]{1,0:T(8,128)(2,1)S(1)} collective-permute-done((bf16[256,1152]{1,0:T(8,128)(2,1)S(1)}, bf16[256,1152]{1,0:T(8,128)(2,1)S(1)}, u32[]{:S(2)}, u32[]{:S(2)}) %collective-permute-start.20) | collective-permute-done | bytes 589856 | tf_op jit(solution)/shard_map/ppermute | solution.py:53
  74.6 2.9 %collective-permute-start.22 = (bf16[64,1152]{1,0:T(8,128)(2,1)S(1)}, bf16[64,1152]{1,0:T(8,128)(2,1)S(1)}, u32[]{:S(2)}, u32[]{:S(2)}) collective-permute-start(bf16[64,1152]{1,0:T(8,128)(2,1)S(1)} %get-tuple-element.42), channel_id=1, source_target_pairs={{0,6},{1,25},{2,0},{3,27},{4,2},{5,29},{6,4},{7,31},{8,14},{9,1},{... | collective-permute-start | bytes 442376 | tf_op jit(solution)/shard_map/ppermute | solution.py:53
  78.5 1.2 %collective-permute-done.26.refs_1_ = bf16[128,1152]{1,0:T(8,128)(2,1)S(1)} collective-permute-done((bf16[128,1152]{1,0:T(8,128)(2,1)S(1)}, bf16[128,1152]{1,0:T(8,128)(2,1)S(1)}, u32[]{:S(2)}, u32[]{:S(2)}) %collective-permute-start.26) | collective-permute-done | bytes 294944 | tf_op jit(solution)/shard_map/ppermute | solution.py:53
  79.7 2.8 %collective-permute-done.25.refs_0_ = bf16[128,1152]{1,0:T(8,128)(2,1)S(1)} collective-permute-done((bf16[128,1152]{1,0:T(8,128)(2,1)S(1)}, bf16[128,1152]{1,0:T(8,128)(2,1)S(1)}, u32[]{:S(2)}, u32[]{:S(2)}) %collective-permute-start.25) | collective-permute-done | bytes 294944 | tf_op jit(solution)/shard_map/ppermute | solution.py:53
  82.5 2.9 %collective-permute-start.27 = (bf16[64,1152]{1,0:T(8,128)(2,1)S(1)}, bf16[64,1152]{1,0:T(8,128)(2,1)S(1)}, u32[]{:S(2)}, u32[]{:S(2)}) collective-permute-start(bf16[64,1152]{1,0:T(8,128)(2,1)S(1)} %add_convert_fusion.1), channel_id=1, source_target_pairs={{0,1},{1,0},{2,3},{3,2},{4,5},{5,4},{6,7},{7,6},{8,9},{9,8},{10,11... | collective-permute-start | bytes 442376 | tf_op jit(solution)/shard_map/ppermute | solution.py:53
  (75 shorter events, 26.2 us)
Async XLA Ops:
  0.6 8.4 %collective-permute-start.3 = (bf16[64,1152]{1,0:T(8,128)(2,1)}, bf16[64,1152]{1,0:T(8,128)(2,1)S(1)}, u32[]{:S(2)}, u32[]{:S(2)}) collective-permute-start(bf16[64,1152]{1,0:T(8,128)(2,1)} %refs_1_.1), channel_id=1, source_target_pairs={{0,1},{1,0},{2,3},{3,2},{4,5},{5,4},{6,7},{7,6},{8,9},{9,8},{10,11... | collective-permute-start | bytes 442376 | tf_op jit(solution)/shard_map/ppermute | solution.py:53
  4.0 11.2 %collective-permute-start = (bf16[64,1152]{1,0:T(8,128)(2,1)}, bf16[64,1152]{1,0:T(8,128)(2,1)S(1)}, u32[]{:S(2)}, u32[]{:S(2)}) collective-permute-start(bf16[64,1152]{1,0:T(8,128)(2,1)} %refs_0_.1), channel_id=1, source_target_pairs={{0,2},{1,9},{2,4},{3,11},{4,6},{5,13},{6,0},{7,15},{8,10},{9,17},{... | collective-permute-start | bytes 442376 | tf_op jit(solution)/shard_map/ppermute | solution.py:53
  4.0 11.2 %collective-permute-start.2 = (bf16[64,1152]{1,0:T(8,128)(2,1)}, bf16[64,1152]{1,0:T(8,128)(2,1)S(1)}, u32[]{:S(2)}, u32[]{:S(2)}) collective-permute-start(bf16[64,1152]{1,0:T(8,128)(2,1)} %refs_0_.1), channel_id=1, source_target_pairs={{0,4},{1,17},{2,6},{3,19},{4,0},{5,21},{6,2},{7,23},{8,12},{9,25},... | collective-permute-start | bytes 442376 | tf_op jit(solution)/shard_map/ppermute | solution.py:53
  6.1 9.1 %collective-permute-start.1 = (bf16[64,1152]{1,0:T(8,128)(2,1)}, bf16[64,1152]{1,0:T(8,128)(2,1)S(1)}, u32[]{:S(2)}, u32[]{:S(2)}) collective-permute-start(bf16[64,1152]{1,0:T(8,128)(2,1)} %refs_0_.1), channel_id=1, source_target_pairs={{0,6},{1,25},{2,0},{3,27},{4,2},{5,29},{6,4},{7,31},{8,14},{9,1},{... | collective-permute-start | bytes 442376 | tf_op jit(solution)/shard_map/ppermute | solution.py:53
  9.1 12.9 %collective-permute-start.4 = (bf16[128,1152]{1,0:T(8,128)(2,1)S(1)}, bf16[128,1152]{1,0:T(8,128)(2,1)S(1)}, u32[]{:S(2)}, u32[]{:S(2)}) collective-permute-start(bf16[128,1152]{1,0:T(8,128)(2,1)S(1)} %join.3), channel_id=1, source_target_pairs={{0,64},{1,193},{2,66},{3,195},{4,68},{5,197},{6,70},{7,199},{8,72}... | collective-permute-start | bytes 884744 | tf_op jit(solution)/shard_map/ppermute | solution.py:53
  15.3 24.4 %collective-permute-start.15 = (bf16[256,1152]{1,0:T(8,128)(2,1)S(1)}, bf16[256,1152]{1,0:T(8,128)(2,1)S(1)}, u32[]{:S(2)}, u32[]{:S(2)}) collective-permute-start(bf16[256,1152]{1,0:T(8,128)(2,1)S(1)} %join.2.refs_0_.raw_ref), channel_id=1, source_target_pairs={{0,16},{1,5},{2,18},{3,7},{4,20},{5,1},{6,22},{7,3},{8,24},{9,13},... | collective-permute-start | bytes 1769480 | tf_op jit(solution)/shard_map/ppermute | solution.py:53
  18.1 22.3 %collective-permute-start.14 = (bf16[256,1152]{1,0:T(8,128)(2,1)S(1)}, bf16[256,1152]{1,0:T(8,128)(2,1)S(1)}, u32[]{:S(2)}, u32[]{:S(2)}) collective-permute-start(bf16[256,1152]{1,0:T(8,128)(2,1)S(1)} %join.2.refs_0_.raw_ref), channel_id=1, source_target_pairs={{0,24},{1,7},{2,26},{3,1},{4,28},{5,3},{6,30},{7,5},{8,0},{9,15},{... | collective-permute-start | bytes 1769480 | tf_op jit(solution)/shard_map/ppermute | solution.py:53
  19.0 6.2 %collective-permute-start.9 = (bf16[128,1152]{1,0:T(8,128)(2,1)S(1)}, bf16[128,1152]{1,0:T(8,128)(2,1)S(1)}, u32[]{:S(2)}, u32[]{:S(2)}) collective-permute-start(bf16[128,1152]{1,0:T(8,128)(2,1)S(1)} %join.3), channel_id=1, source_target_pairs={{0,32},{1,225},{2,34},{3,227},{4,36},{5,229},{6,38},{7,231},{8,40}... | collective-permute-start | bytes 884744 | tf_op jit(solution)/shard_map/ppermute | solution.py:53
  20.0 21.0 %collective-permute-start.13 = (bf16[256,1152]{1,0:T(8,128)(2,1)S(1)}, bf16[256,1152]{1,0:T(8,128)(2,1)S(1)}, u32[]{:S(2)}, u32[]{:S(2)}) collective-permute-start(bf16[256,1152]{1,0:T(8,128)(2,1)S(1)} %join.2.refs_0_.raw_ref), channel_id=1, source_target_pairs={{0,8},{1,3},{2,10},{3,5},{4,12},{5,7},{6,14},{7,1},{8,16},{9,11},{... | collective-permute-start | bytes 1769480 | tf_op jit(solution)/shard_map/ppermute | solution.py:53
  22.0 17.6 %collective-permute-start.5 = (bf16[128,1152]{1,0:T(8,128)(2,1)S(1)}, bf16[128,1152]{1,0:T(8,128)(2,1)S(1)}, u32[]{:S(2)}, u32[]{:S(2)}) collective-permute-start(bf16[128,1152]{1,0:T(8,128)(2,1)S(1)} %collective-permute-done.4.src.refs_5_.refs_9_), channel_id=1, source_target_pairs={{0,32},{1,225},{2,34},{3,227},{4,36},{5,229},{6,38},{7,231},{8,40}... | collective-permute-start | bytes 884744 | tf_op jit(solution)/shard_map/ppermute | solution.py:53
  25.2 4.1 %collective-permute-start.12 = (s32[8,128]{1,0:T(8,128)S(1)}, s32[8,128]{1,0:T(8,128)S(1)}, u32[]{:S(2)}, u32[]{:S(2)}) collective-permute-start(s32[8,128]{1,0:T(8,128)S(1)} %bitcast.51), channel_id=1, source_target_pairs={{0,16},{1,17},{2,18},{3,19},{4,20},{5,21},{6,22},{7,23},{8,24},{9,... | collective-permute-start | bytes 12296 | tf_op jit(solution)/shard_map/ppermute | solution.py:53
  29.3 6.3 %collective-permute-start.6 = (bf16[64,1152]{1,0:T(8,128)(2,1)}, bf16[64,1152]{1,0:T(8,128)(2,1)}, u32[]{:S(2)}, u32[]{:S(2)}) collective-permute-start(bf16[64,1152]{1,0:T(8,128)(2,1)} %head.1), channel_id=1, source_target_pairs={{0,64},{1,193},{2,66},{3,195},{4,68},{5,197},{6,70},{7,199},{8,72}... | collective-permute-start | bytes 442376 | tf_op jit(solution)/shard_map/ppermute | solution.py:53
  35.6 6.6 %collective-permute-start.11 = (bf16[128,1152]{1,0:T(8,128)(2,1)S(1)}, bf16[128,1152]{1,0:T(8,128)(2,1)S(1)}, u32[]{:S(2)}, u32[]{:S(2)}) collective-permute-start(bf16[128,1152]{1,0:T(8,128)(2,1)S(1)} %collective-permute-done.4.src.refs_5_.refs_9_), channel_id=1, source_target_pairs={{0,1},{1,0},{2,3},{3,2},{4,5},{5,4},{6,7},{7,6},{8,9},{9,8},{10,11... | collective-permute-start | bytes 884744 | tf_op jit(solution)/shard_map/ppermute | solution.py:53
  51.9 15.7 %collective-permute-start.18 = (bf16[192,1152]{1,0:T(8,128)(2,1)S(1)}, bf16[192,1152]{1,0:T(8,128)(2,1)S(1)}, u32[]{:S(2)}, u32[]{:S(2)}) collective-permute-start(bf16[192,1152]{1,0:T(8,128)(2,1)S(1)} %add_convert_fusion), channel_id=1, source_target_pairs={{0,64},{1,193},{2,66},{3,195},{4,68},{5,197},{6,70},{7,199},{8,72}... | collective-permute-start | bytes 1327112 | tf_op jit(solution)/shard_map/ppermute | solution.py:53
  57.2 10.5 %collective-permute-start.17 = (bf16[320,1152]{1,0:T(8,128)(2,1)S(1)}, bf16[320,1152]{1,0:T(8,128)(2,1)S(1)}, u32[]{:S(2)}, u32[]{:S(2)}) collective-permute-start(bf16[320,1152]{1,0:T(8,128)(2,1)S(1)} %near_give.1), channel_id=1, source_target_pairs={{0,1},{1,0},{2,3},{3,2},{4,5},{5,4},{6,7},{7,6},{8,9},{9,8},{10,11... | collective-permute-start | bytes 2211848 | tf_op jit(solution)/shard_map/ppermute | solution.py:53
  57.3 16.9 %collective-permute-start.21 = (bf16[256,1152]{1,0:T(8,128)(2,1)S(1)}, bf16[256,1152]{1,0:T(8,128)(2,1)S(1)}, u32[]{:S(2)}, u32[]{:S(2)}) collective-permute-start(bf16[256,1152]{1,0:T(8,128)(2,1)S(1)} %image_sum.5), channel_id=1, source_target_pairs={{0,16},{1,5},{2,18},{3,7},{4,20},{5,1},{6,22},{7,3},{8,24},{9,13},... | collective-permute-start | bytes 1769480 | tf_op jit(solution)/shard_map/ppermute | solution.py:53
  60.8 13.4 %collective-permute-start.20 = (bf16[256,1152]{1,0:T(8,128)(2,1)S(1)}, bf16[256,1152]{1,0:T(8,128)(2,1)S(1)}, u32[]{:S(2)}, u32[]{:S(2)}) collective-permute-start(bf16[256,1152]{1,0:T(8,128)(2,1)S(1)} %image_sum.7), channel_id=1, source_target_pairs={{0,8},{1,3},{2,10},{3,5},{4,12},{5,7},{6,14},{7,1},{8,16},{9,11},{... | collective-permute-start | bytes 1769480 | tf_op jit(solution)/shard_map/ppermute | solution.py:53
  63.0 11.2 %collective-permute-start.19 = (bf16[256,1152]{1,0:T(8,128)(2,1)S(1)}, bf16[256,1152]{1,0:T(8,128)(2,1)S(1)}, u32[]{:S(2)}, u32[]{:S(2)}) collective-permute-start(bf16[256,1152]{1,0:T(8,128)(2,1)S(1)} %image_sum.6), channel_id=1, source_target_pairs={{0,24},{1,7},{2,26},{3,1},{4,28},{5,3},{6,30},{7,5},{8,0},{9,15},{... | collective-permute-start | bytes 1769480 | tf_op jit(solution)/shard_map/ppermute | solution.py:53
  68.0 11.7 %collective-permute-start.26 = (bf16[128,1152]{1,0:T(8,128)(2,1)S(1)}, bf16[128,1152]{1,0:T(8,128)(2,1)S(1)}, u32[]{:S(2)}, u32[]{:S(2)}) collective-permute-start(bf16[128,1152]{1,0:T(8,128)(2,1)S(1)} %pad_maximum_fusion), channel_id=1, source_target_pairs={{0,64},{1,193},{2,66},{3,195},{4,68},{5,197},{6,70},{7,199},{8,72}... | collective-permute-start | bytes 884744 | tf_op jit(solution)/shard_map/ppermute | solution.py:53
  71.8 10.6 %collective-permute-start.25 = (bf16[128,1152]{1,0:T(8,128)(2,1)S(1)}, bf16[128,1152]{1,0:T(8,128)(2,1)S(1)}, u32[]{:S(2)}, u32[]{:S(2)}) collective-permute-start(bf16[128,1152]{1,0:T(8,128)(2,1)S(1)} %slice.46), channel_id=1, source_target_pairs={{0,32},{1,225},{2,34},{3,227},{4,36},{5,229},{6,38},{7,231},{8,40}... | collective-permute-start | bytes 884744 | tf_op jit(solution)/shard_map/ppermute | solution.py:53
  74.6 10.9 %collective-permute-start.22 = (bf16[64,1152]{1,0:T(8,128)(2,1)S(1)}, bf16[64,1152]{1,0:T(8,128)(2,1)S(1)}, u32[]{:S(2)}, u32[]{:S(2)}) collective-permute-start(bf16[64,1152]{1,0:T(8,128)(2,1)S(1)} %get-tuple-element.42), channel_id=1, source_target_pairs={{0,6},{1,25},{2,0},{3,27},{4,2},{5,29},{6,4},{7,31},{8,14},{9,1},{... | collective-permute-start | bytes 442376 | tf_op jit(solution)/shard_map/ppermute | solution.py:53
  77.4 8.0 %collective-permute-start.24 = (bf16[64,1152]{1,0:T(8,128)(2,1)S(1)}, bf16[64,1152]{1,0:T(8,128)(2,1)S(1)}, u32[]{:S(2)}, u32[]{:S(2)}) collective-permute-start(bf16[64,1152]{1,0:T(8,128)(2,1)S(1)} %get-tuple-element.43), channel_id=1, source_target_pairs={{0,4},{1,17},{2,6},{3,19},{4,0},{5,21},{6,2},{7,23},{8,12},{9,25},... | collective-permute-start | bytes 442376 | tf_op jit(solution)/shard_map/ppermute | solution.py:53
  77.8 7.7 %collective-permute-start.23 = (bf16[64,1152]{1,0:T(8,128)(2,1)S(1)}, bf16[64,1152]{1,0:T(8,128)(2,1)S(1)}, u32[]{:S(2)}, u32[]{:S(2)}) collective-permute-start(bf16[64,1152]{1,0:T(8,128)(2,1)S(1)} %get-tuple-element.44), channel_id=1, source_target_pairs={{0,2},{1,9},{2,4},{3,11},{4,6},{5,13},{6,0},{7,15},{8,10},{9,17},{... | collective-permute-start | bytes 442376 | tf_op jit(solution)/shard_map/ppermute | solution.py:53
  82.5 3.9 %collective-permute-start.27 = (bf16[64,1152]{1,0:T(8,128)(2,1)S(1)}, bf16[64,1152]{1,0:T(8,128)(2,1)S(1)}, u32[]{:S(2)}, u32[]{:S(2)}) collective-permute-start(bf16[64,1152]{1,0:T(8,128)(2,1)S(1)} %add_convert_fusion.1), channel_id=1, source_target_pairs={{0,1},{1,0},{2,3},{3,2},{4,5},{5,4},{6,7},{7,6},{8,9},{9,8},{10,11... | collective-permute-start | bytes 442376 | tf_op jit(solution)/shard_map/ppermute | solution.py:53
  (7 other events, 25.9 us)
where the time goes:
time: 87.9 us; the launch traced here: 87.2 us
  starting transfers between devices  48.4 us (55%)
  Pallas kernels  18.3 us (21%)
  waiting for transfers between devices  14.4 us (16%)
  other arithmetic  2.17 us (2%)
  local copies, waits for them, and re-layouts  2.05 us (2%)
  between operations  1.78 us (2%)
    ppermute x28, starting transfers between devices, send(): return lax.ppermute(v, AXES, perm)  48.4 us
    ppermute x28, waiting for transfers between devices, send(): return lax.ppermute(v, AXES, perm)  14.4 us
    pallas_call x4, Pallas kernels, text_sum(): pl.pallas_call(functools.partial(text_kernel, first), out_shape=sds((rows...  5.47 us
    pallas_call x4, Pallas kernels, image_sum(): pl.pallas_call(image_kernel, out_shape=sds(raw.shape, BF16), in_specs=[VM...  4.74 us
    pallas_call x4, Pallas kernels, tile(): pl.pallas_call(functools.partial(tile_kernel, quarter), out_shape=sds((yh...  4.14 us
    pallas_call x5, Pallas kernels, normalize(): pl.pallas_call(norm_kernel, out_shape=sds((rows, width), BF16), in_specs=...  2.45 us
    unnamed x6, local copies, waits for them, and re-layouts  1.82 us
  transfers between devices with their start and end apart: 28, of which 11 were waited for; matrix products, arithmetic and copies ran while one was open for 2% of the time, Pallas kernels for 12%

commit v1 on v0

--- a/solution.py
+++ b/solution.py
@@ -127,7 +127,7 @@
     out_ref[...] = project(raw_ref[...], d_ref[...])
 
 
-def text_kernel(first, *refs):
+def text_kernel(first, spans, *refs):
     gs, xs, pieces = refs[:4], refs[4:8], refs[8:-2]
     out_ref, d_ref = refs[-2:]
     rows, width = out_ref.shape
@@ -140,9 +140,9 @@
             total = part if total is None else total + part
         d_ref[:, n : n + 384] = total
     row = 0
-    for p in pieces:
-        n = p.shape[0]
-        out_ref[row : row + n, :] = project(p[...], d_ref[row : row + n, :])
+    for p, (low, high) in zip(pieces, spans):
+        n = high - low
+        out_ref[row : row + n, :] = project(p[low:high, :], d_ref[row : row + n, :])
         row += n
 
 
@@ -266,18 +266,20 @@
 
 
 def text_sum(first, gs, xs, pieces, name):
-    rows = sum(p.shape[0] for p in pieces)
-    width = pieces[0].shape[1]
-    return pl.pallas_call(
-        functools.partial(text_kernel, first),
+    arrays = [p[0] for p in pieces]
+    spans = tuple((low, high) for _, low, high in pieces)
+    rows = sum(high - low for low, high in spans)
+    width = arrays[0].shape[1]
+    return pl.pallas_call(
+        functools.partial(text_kernel, first, spans),
         out_shape=sds((rows, width), BF16),
-        in_specs=[VM] * (8 + len(pieces)),
+        in_specs=[VM] * (8 + len(arrays)),
         out_specs=VM,
         scratch_shapes=[pltpu.VMEM((rows, width), F32)],
         compiler_params=PARAMS,
         cost_estimate=cost(rows / 230),
         name=name,
-    )(*fast(*gs, *xs, *pieces))
+    )(*fast(*gs, *xs, *arrays))
 
 
 def add(*terms):
@@ -300,12 +302,15 @@
     chip = join(text_emb, other)
     one = send(chip, Z_ONE)
     two = send(chip, Z_TWO)
+    three = send(two, Z_ONE)
+    four = send(head(two, 64), Z_TWO)
+
     def text_base(zz, cc):
         return ((((yl * 4 + x) * 2 + cc) * 8 + zz % 8) * 2 + yh) * 64
 
     at = [(z - 3 * s, c), (z - 3 * s, d), (z + 4, c)]
+    at += [(z - s, c), (z - s, d), (z - 2 * s, c), (z - 2 * s, d), (z, d)]
     at += [(z + 3 * s, d), (z + 3 * s, c), (z + 4, d)]
-    at += [(z - s, c), (z - s, d), (z - 2 * s, c), (z - 2 * s, d), (z, d)]
     at += [(z + s, d), (z + s, c), (z + 2 * s, d), (z + 2 * s, c), (z, c)]
     table = [text_base(*p) for p in at]
     rows, mine = [], []
@@ -318,26 +323,24 @@
     tab = jnp.stack([v.astype(jnp.int32) for v in table + rows + mine + [c]])
     scale = (loss_scale * (temper / 16384.0)).reshape(1)
     own_pairs = positive.reshape(8, 128)
-    own_pairs, two = lax.optimization_barrier((own_pairs, two))
+    own_pairs, three = lax.optimization_barrier((own_pairs, three))
     across_pairs = send(own_pairs, Y_TWO)
     pos, ids, weight = setup(tab, scale, own_pairs, across_pairs)
 
-    three = send(two, Z_ONE)
-    four = send(head(two, 64), Z_TWO)
-    far_give = [three, four]
-    far_keep = [send(three, CORE), send(four, CORE)]
-    near_give = [one, two, other]
-    near_keep = [send(one, CORE), send(two, CORE), text_emb]
+    give = join(three, four, one, two)
+    keep = send(give, CORE)
+    far_give, near_give = [(give, 0, 192)], [(give, 192, 448), (other, 0, 64)]
+    far_keep, near_keep = [(keep, 0, 192)], [(keep, 192, 448), (text_emb, 0, 64)]
 
     row = join(images, send(image_emb, A_ON), send(image_emb, A_BACK), send(image_emb, A_TWO))
     quarters = [row, send(row, B_ON), send(row, B_BACK), send(row, B_TWO)]
-    xs = [normalize(quarters[0], us=0.3)] + [normalize(q, us=10) for q in quarters[1:]]
-
-    yh_all = normalize(*far_give, *far_keep, *near_give, *near_keep)
+    xs = [normalize(quarters[0], us=0.3)] + [normalize(q, us=40) for q in quarters[1:]]
+
+    yh_all = normalize(give, other, keep, text_emb)
     gs = [tile(k, weight, pos, ids, xs[k], yh_all) for k in range(4)]
     d_give = text_sum(0, gs, xs, far_give, "far_give")
     swapped = send(d_give, CORE)
-    d_keep = text_sum(192, gs, xs, far_keep, "far_keep")
+    d_keep = text_sum(512, gs, xs, far_keep, "far_keep")
     far_sum = add(d_keep, swapped).astype(BF16)
     relay = send(far_sum, Z_TWO)
 
@@ -346,7 +349,7 @@
     back = [send(es[1], B_BACK), send(es[2], B_ON), send(es[3], B_TWO)]
 
     _, *gs = lax.optimization_barrier((es[3], *gs))
-    d_give = text_sum(384, gs, xs, near_give, "near_give")
+    d_give = text_sum(192, gs, xs, near_give, "near_give")
     swapped = send(d_give, CORE)
     d_keep = text_sum(704, gs, xs, near_keep, "near_keep")
     near_sum = add(d_keep, swapped)

time: 87.9 us -> 85.3 us (0.970)
  starting transfers between devices: 48.4 us -> 40.5 us
  waiting for transfers between devices: 14.4 us -> 20.8 us
  Pallas kernels: 18.3 us -> 15.9 us
  between operations: 1.78 us -> 3.33 us
    ppermute x28 -> x25, starting transfers between devices: 48.4 us -> 40.5 us  [send(): return lax.ppermute(v, AXES, perm)]
    ppermute x28 -> x25, waiting for transfers between devices: 14.4 us -> 20.8 us  [send(): return lax.ppermute(v, AXES, perm)]
    pallas_call x5, Pallas kernels: 2.45 us -> 1.54 us  [normalize(): pl.pallas_call(norm_kernel, out_shape=sds((rows, width), BF16), in_specs=...]
    pallas_call x4, Pallas kernels: 5.47 us -> 4.56 us  [text_sum(): pl.pallas_call(functools.partial(text_kernel, first, spans), out_shape=sd...]
  transfers between devices with their start and end apart: 28 -> 25, of which waited for: 11 -> 8; matrix products, arithmetic and copies ran while one was open for 2% -> 2% of each run, Pallas kernels for 12% -> 12%
where the time goes in v1:
time: 85.3 us; the launch traced here: 84.7 us
  starting transfers between devices  40.5 us (47%)
  waiting for transfers between devices  20.8 us (24%)
  Pallas kernels  15.9 us (19%)
  between operations  3.33 us (4%)
  other arithmetic  2.14 us (3%)
  local copies, waits for them, and re-layouts  2.05 us (2%)
    ppermute x25, starting transfers between devices, send(): return lax.ppermute(v, AXES, perm)  40.5 us
    ppermute x25, waiting for transfers between devices, send(): return lax.ppermute(v, AXES, perm)  20.8 us
    pallas_call x4, Pallas kernels, image_sum(): pl.pallas_call(image_kernel, out_shape=sds(raw.shape, BF16), in_specs=[VM...  4.74 us
    pallas_call x4, Pallas kernels, text_sum(): pl.pallas_call(functools.partial(text_kernel, first, spans), out_shape=sd...  4.56 us
    pallas_call x4, Pallas kernels, tile(): pl.pallas_call(functools.partial(tile_kernel, quarter), out_shape=sds((yh...  4.13 us
    unnamed x6, local copies, waits for them, and re-layouts  1.83 us
  transfers between devices with their start and end apart: 25, of which 8 were waited for; matrix products, arithmetic and copies ran while one was open for 2% of the time, Pallas kernels for 12%

profile of v1, /device:TPU:1, one launch (start us, length us, event | category | flops | bytes accessed | tf_op | source)
XLA Modules:
  0.0 84.7 jit_solution(11072724534836491431)
XLA Ops:
  0.6 3.3 %collective-permute-start.3 = (bf16[64,1152]{1,0:T(8,128)(2,1)}, bf16[64,1152]{1,0:T(8,128)(2,1)S(1)}, u32[]{:S(2)}, u32[]{:S(2)}) collective-permute-start(bf16[64,1152]{1,0:T(8,128)(2,1)} %refs_1_.1), channel_id=1, source_target_pairs={{0,1},{1,0},{2,3},{3,2},{4,5},{5,4},{6,7},{7,6},{8,9},{9,8},{10,11... | collective-permute-start | bytes 442376 | tf_op jit(solution)/shard_map/ppermute | solution.py:53
  4.0 2.2 %collective-permute-start.2 = (bf16[64,1152]{1,0:T(8,128)(2,1)}, bf16[64,1152]{1,0:T(8,128)(2,1)S(1)}, u32[]{:S(2)}, u32[]{:S(2)}) collective-permute-start(bf16[64,1152]{1,0:T(8,128)(2,1)} %refs_0_.1), channel_id=1, source_target_pairs={{0,4},{1,17},{2,6},{3,19},{4,0},{5,21},{6,2},{7,23},{8,12},{9,25},... | collective-permute-start | bytes 442376 | tf_op jit(solution)/shard_map/ppermute | solution.py:53
  9.1 6.1 %collective-permute-start.4 = (bf16[128,1152]{1,0:T(8,128)(2,1)S(1)}, bf16[128,1152]{1,0:T(8,128)(2,1)S(1)}, u32[]{:S(2)}, u32[]{:S(2)}) collective-permute-start(bf16[128,1152]{1,0:T(8,128)(2,1)S(1)} %join.4), channel_id=1, source_target_pairs={{0,64},{1,193},{2,66},{3,195},{4,68},{5,197},{6,70},{7,199},{8,72}... | collective-permute-start | bytes 884744 | tf_op jit(solution)/shard_map/ppermute | solution.py:53
  15.3 2.8 %collective-permute-start.12 = (bf16[256,1152]{1,0:T(8,128)(2,1)S(1)}, bf16[256,1152]{1,0:T(8,128)(2,1)S(1)}, u32[]{:S(2)}, u32[]{:S(2)}) collective-permute-start(bf16[256,1152]{1,0:T(8,128)(2,1)S(1)} %join.3.refs_0_.raw_ref), channel_id=1, source_target_pairs={{0,16},{1,5},{2,18},{3,7},{4,20},{5,1},{6,22},{7,3},{8,24},{9,13},... | collective-permute-start | bytes 1769480 | tf_op jit(solution)/shard_map/ppermute | solution.py:53
  18.1 3.9 %collective-permute-done.4.src.refs_3_ = bf16[128,1152]{1,0:T(8,128)(2,1)S(1)} collective-permute-done((bf16[128,1152]{1,0:T(8,128)(2,1)S(1)}, bf16[128,1152]{1,0:T(8,128)(2,1)S(1)}, u32[]{:S(2)}, u32[]{:S(2)}) %collective-permute-start.4) | collective-permute-done | bytes 294944 | tf_op jit(solution)/shard_map/ppermute | solution.py:53
  22.0 2.4 %collective-permute-start.5 = (bf16[128,1152]{1,0:T(8,128)(2,1)S(1)}, bf16[128,1152]{1,0:T(8,128)(2,1)S(1)}, u32[]{:S(2)}, u32[]{:S(2)}) collective-permute-start(bf16[128,1152]{1,0:T(8,128)(2,1)S(1)} %collective-permute-done.4.src.refs_3_), channel_id=1, source_target_pairs={{0,32},{1,225},{2,34},{3,227},{4,36},{5,229},{6,38},{7,231},{8,40}... | collective-permute-start | bytes 884744 | tf_op jit(solution)/shard_map/ppermute | solution.py:53
  24.4 2.2 %collective-permute-start.7 = (bf16[128,1152]{1,0:T(8,128)(2,1)S(1)}, bf16[128,1152]{1,0:T(8,128)(2,1)S(1)}, u32[]{:S(2)}, u32[]{:S(2)}) collective-permute-start(bf16[128,1152]{1,0:T(8,128)(2,1)S(1)} %join.4), channel_id=1, source_target_pairs={{0,32},{1,225},{2,34},{3,227},{4,36},{5,229},{6,38},{7,231},{8,40}... | collective-permute-start | bytes 884744 | tf_op jit(solution)/shard_map/ppermute | solution.py:53
  26.6 2.5 %collective-permute-start.11 = (bf16[256,1152]{1,0:T(8,128)(2,1)S(1)}, bf16[256,1152]{1,0:T(8,128)(2,1)S(1)}, u32[]{:S(2)}, u32[]{:S(2)}) collective-permute-start(bf16[256,1152]{1,0:T(8,128)(2,1)S(1)} %join.3.refs_0_.raw_ref), channel_id=1, source_target_pairs={{0,24},{1,7},{2,26},{3,1},{4,28},{5,3},{6,30},{7,5},{8,0},{9,15},{... | collective-permute-start | bytes 1769480 | tf_op jit(solution)/shard_map/ppermute | solution.py:53
  33.7 2.1 %collective-permute-done.6.refs_1_ = bf16[64,1152]{1,0:T(8,128)(2,1)S(1)} collective-permute-done((bf16[64,1152]{1,0:T(8,128)(2,1)S(1)}, bf16[64,1152]{1,0:T(8,128)(2,1)S(1)}, u32[]{:S(2)}, u32[]{:S(2)}) %collective-permute-start.6) | collective-permute-done | bytes 147488 | tf_op jit(solution)/shard_map/ppermute | solution.py:53
  35.9 2.2 %collective-permute-start.8 = (bf16[448,1152]{1,0:T(8,128)(2,1)S(1)}, bf16[448,1152]{1,0:T(8,128)(2,1)S(1)}, u32[]{:S(2)}, u32[]{:S(2)}) collective-permute-start(bf16[448,1152]{1,0:T(8,128)(2,1)S(1)} %join.5.refs_0_.refs_8_), channel_id=1, source_target_pairs={{0,1},{1,0},{2,3},{3,2},{4,5},{5,4},{6,7},{7,6},{8,9},{9,8},{10,11... | collective-permute-start | bytes 3096584 | tf_op jit(solution)/shard_map/ppermute | solution.py:53
  38.5 3.7 %collective-permute-done.10.refs_0_.raw_ref = bf16[256,1152]{1,0:T(8,128)(2,1)S(1)} collective-permute-done((bf16[256,1152]{1,0:T(8,128)(2,1)S(1)}, bf16[256,1152]{1,0:T(8,128)(2,1)S(1)}, u32[]{:S(2)}, u32[]{:S(2)}) %collective-permute-start.10) | collective-permute-done | bytes 589856 | tf_op jit(solution)/shard_map/ppermute | solution.py:53
  49.0 3.5 %collective-permute-start.13 = (bf16[192,1152]{1,0:T(8,128)(2,1)S(1)}, bf16[192,1152]{1,0:T(8,128)(2,1)S(1)}, u32[]{:S(2)}, u32[]{:S(2)}) collective-permute-start(bf16[192,1152]{1,0:T(8,128)(2,1)S(1)} %far_give.1), channel_id=1, source_target_pairs={{0,1},{1,0},{2,3},{3,2},{4,5},{5,4},{6,7},{7,6},{8,9},{9,8},{10,11... | collective-permute-start | bytes 1327112 | tf_op jit(solution)/shard_map/ppermute | solution.py:53
  54.2 1.2 %image_sum.5 = bf16[256,1152]{1,0:T(8,128)(2,1)S(1)} custom-call(bf16[256,1152]{1,0:T(8,128)(2,1)S(1)} %collective-permute-done.12.refs_0_.raw_ref, bf16[1024,1152]{1,0:T(8,128)(2,1)S(1)} %normalize.5.yh_ref, bf16[1024,256]{1,0:T(8,128)(2,1)S(1)} %tile.7.refs_3_.g_ref), custom_call_target="tpu_custom_call" | custom-call | flops 184000000 | bytes 1 | tf_op jit(solution)/shard_map/image_sum/pallas_call | solution.py:256
  55.4 1.4 %near_give.1 = bf16[320,1152]{1,0:T(8,128)(2,1)S(1)} custom-call(bf16[1024,256]{1,0:T(8,128)(2,1)S(1)} %tile.4.refs_0_.g_ref, bf16[1024,256]{1,0:T(8,128)(2,1)S(1)} %tile.5.refs_1_.g_ref, bf16[1024,256]{1,0:T(8,128)(2,1)S(1)} %tile.6.refs_2_.g_ref, bf16[1024,256]{1,0:T(8,128)(2,1)S(1)} %tile.7.refs_3_.g_ref, bf16[256,1152]{1,0:T(8,128)(2,1)S(1)} %normalize.6.xh_ref.refs_4_, ...), custom_call_target="tpu_custom_call" | custom-call | flops 160000000 | bytes 1 | tf_op jit(solution)/shard_map/near_give/pallas_call | solution.py:273
  56.7 2.0 %collective-permute-start.14 = (bf16[320,1152]{1,0:T(8,128)(2,1)S(1)}, bf16[320,1152]{1,0:T(8,128)(2,1)S(1)}, u32[]{:S(2)}, u32[]{:S(2)}) collective-permute-start(bf16[320,1152]{1,0:T(8,128)(2,1)S(1)} %near_give.1), channel_id=1, source_target_pairs={{0,1},{1,0},{2,3},{3,2},{4,5},{5,4},{6,7},{7,6},{8,9},{9,8},{10,11... | collective-permute-start | bytes 2211848 | tf_op jit(solution)/shard_map/ppermute | solution.py:53
  58.9 1.2 %image_sum.7 = bf16[256,1152]{1,0:T(8,128)(2,1)S(1)} custom-call(bf16[256,1152]{1,0:T(8,128)(2,1)S(1)} %collective-permute-done.11.refs_0_.raw_ref, bf16[1024,1152]{1,0:T(8,128)(2,1)S(1)} %normalize.5.yh_ref, bf16[1024,256]{1,0:T(8,128)(2,1)S(1)} %tile.6.refs_2_.g_ref), custom_call_target="tpu_custom_call" | custom-call | flops 184000000 | bytes 1 | tf_op jit(solution)/shard_map/image_sum/pallas_call | solution.py:256
  61.7 2.7 %collective-permute-start.16 = (bf16[256,1152]{1,0:T(8,128)(2,1)S(1)}, bf16[256,1152]{1,0:T(8,128)(2,1)S(1)}, u32[]{:S(2)}, u32[]{:S(2)}) collective-permute-start(bf16[256,1152]{1,0:T(8,128)(2,1)S(1)} %image_sum.6), channel_id=1, source_target_pairs={{0,24},{1,7},{2,26},{3,1},{4,28},{5,3},{6,30},{7,5},{8,0},{9,15},{... | collective-permute-start | bytes 1769480 | tf_op jit(solution)/shard_map/ppermute | solution.py:53
  64.4 1.4 %near_keep.1 = bf16[320,1152]{1,0:T(8,128)(2,1)S(1)} custom-call(bf16[1024,256]{1,0:T(8,128)(2,1)S(1)} %tile.4.refs_0_.g_ref, bf16[1024,256]{1,0:T(8,128)(2,1)S(1)} %tile.5.refs_1_.g_ref, bf16[1024,256]{1,0:T(8,128)(2,1)S(1)} %tile.6.refs_2_.g_ref, bf16[1024,256]{1,0:T(8,128)(2,1)S(1)} %tile.7.refs_3_.g_ref, bf16[256,1152]{1,0:T(8,128)(2,1)S(1)} %normalize.6.xh_ref.refs_4_, ...), custom_call_target="tpu_custom_call" | custom-call | flops 160000000 | bytes 1 | tf_op jit(solution)/shard_map/near_keep/pallas_call | solution.py:273
  65.7 1.2 %image_sum.4 = bf16[256,1152]{1,0:T(8,128)(2,1)S(1)} custom-call(bf16[256,1152]{1,0:T(8,128)(2,1)S(1)} %join.3.refs_0_.raw_ref, bf16[1024,1152]{1,0:T(8,128)(2,1)S(1)} %normalize.5.yh_ref, bf16[1024,256]{1,0:T(8,128)(2,1)S(1)} %tile.4.refs_0_.g_ref), custom_call_target="tpu_custom_call" | custom-call | flops 184000000 | bytes 1 | tf_op jit(solution)/shard_map/image_sum/pallas_call | solution.py:256
  67.3 2.4 %collective-permute-start.23 = (bf16[128,1152]{1,0:T(8,128)(2,1)S(1)}, bf16[128,1152]{1,0:T(8,128)(2,1)S(1)}, u32[]{:S(2)}, u32[]{:S(2)}) collective-permute-start(bf16[128,1152]{1,0:T(8,128)(2,1)S(1)} %pad_maximum_fusion), channel_id=1, source_target_pairs={{0,64},{1,193},{2,66},{3,195},{4,68},{5,197},{6,70},{7,199},{8,72}... | collective-permute-start | bytes 884744 | tf_op jit(solution)/shard_map/ppermute | solution.py:53
  69.8 5.8 %collective-permute-done.17 = bf16[256,1152]{1,0:T(8,128)(2,1)S(1)} collective-permute-done((bf16[256,1152]{1,0:T(8,128)(2,1)S(1)}, bf16[256,1152]{1,0:T(8,128)(2,1)S(1)}, u32[]{:S(2)}, u32[]{:S(2)}) %collective-permute-start.17) | collective-permute-done | bytes 589856 | tf_op jit(solution)/shard_map/ppermute | solution.py:53
  76.2 1.2 %collective-permute-start.20 = (bf16[64,1152]{1,0:T(8,128)(2,1)S(1)}, bf16[64,1152]{1,0:T(8,128)(2,1)S(1)}, u32[]{:S(2)}, u32[]{:S(2)}) collective-permute-start(bf16[64,1152]{1,0:T(8,128)(2,1)S(1)} %get-tuple-element.44), channel_id=1, source_target_pairs={{0,2},{1,9},{2,4},{3,11},{4,6},{5,13},{6,0},{7,15},{8,10},{9,17},{... | collective-permute-start | bytes 442376 | tf_op jit(solution)/shard_map/ppermute | solution.py:53
  77.4 2.8 %collective-permute-done.22.refs_0_ = bf16[128,1152]{1,0:T(8,128)(2,1)S(1)} collective-permute-done((bf16[128,1152]{1,0:T(8,128)(2,1)S(1)}, bf16[128,1152]{1,0:T(8,128)(2,1)S(1)}, u32[]{:S(2)}, u32[]{:S(2)}) %collective-permute-start.22) | collective-permute-done | bytes 294944 | tf_op jit(solution)/shard_map/ppermute | solution.py:53
  80.3 1.9 %collective-permute-start.24 = (bf16[64,1152]{1,0:T(8,128)(2,1)S(1)}, bf16[64,1152]{1,0:T(8,128)(2,1)S(1)}, u32[]{:S(2)}, u32[]{:S(2)}) collective-permute-start(bf16[64,1152]{1,0:T(8,128)(2,1)S(1)} %add_convert_fusion.1), channel_id=1, source_target_pairs={{0,1},{1,0},{2,3},{3,2},{4,5},{5,4},{6,7},{7,6},{8,9},{9,8},{10,11... | collective-permute-start | bytes 442376 | tf_op jit(solution)/shard_map/ppermute | solution.py:53
  (70 shorter events, 19.4 us)
Async XLA Ops:
  0.6 8.4 %collective-permute-start.3 = (bf16[64,1152]{1,0:T(8,128)(2,1)}, bf16[64,1152]{1,0:T(8,128)(2,1)S(1)}, u32[]{:S(2)}, u32[]{:S(2)}) collective-permute-start(bf16[64,1152]{1,0:T(8,128)(2,1)} %refs_1_.1), channel_id=1, source_target_pairs={{0,1},{1,0},{2,3},{3,2},{4,5},{5,4},{6,7},{7,6},{8,9},{9,8},{10,11... | collective-permute-start | bytes 442376 | tf_op jit(solution)/shard_map/ppermute | solution.py:53
  4.0 11.2 %collective-permute-start = (bf16[64,1152]{1,0:T(8,128)(2,1)}, bf16[64,1152]{1,0:T(8,128)(2,1)S(1)}, u32[]{:S(2)}, u32[]{:S(2)}) collective-permute-start(bf16[64,1152]{1,0:T(8,128)(2,1)} %refs_0_.1), channel_id=1, source_target_pairs={{0,2},{1,9},{2,4},{3,11},{4,6},{5,13},{6,0},{7,15},{8,10},{9,17},{... | collective-permute-start | bytes 442376 | tf_op jit(solution)/shard_map/ppermute | solution.py:53
  4.0 11.2 %collective-permute-start.2 = (bf16[64,1152]{1,0:T(8,128)(2,1)}, bf16[64,1152]{1,0:T(8,128)(2,1)S(1)}, u32[]{:S(2)}, u32[]{:S(2)}) collective-permute-start(bf16[64,1152]{1,0:T(8,128)(2,1)} %refs_0_.1), channel_id=1, source_target_pairs={{0,4},{1,17},{2,6},{3,19},{4,0},{5,21},{6,2},{7,23},{8,12},{9,25},... | collective-permute-start | bytes 442376 | tf_op jit(solution)/shard_map/ppermute | solution.py:53
  6.1 9.1 %collective-permute-start.1 = (bf16[64,1152]{1,0:T(8,128)(2,1)}, bf16[64,1152]{1,0:T(8,128)(2,1)S(1)}, u32[]{:S(2)}, u32[]{:S(2)}) collective-permute-start(bf16[64,1152]{1,0:T(8,128)(2,1)} %refs_0_.1), channel_id=1, source_target_pairs={{0,6},{1,25},{2,0},{3,27},{4,2},{5,29},{6,4},{7,31},{8,14},{9,1},{... | collective-permute-start | bytes 442376 | tf_op jit(solution)/shard_map/ppermute | solution.py:53
  9.1 12.9 %collective-permute-start.4 = (bf16[128,1152]{1,0:T(8,128)(2,1)S(1)}, bf16[128,1152]{1,0:T(8,128)(2,1)S(1)}, u32[]{:S(2)}, u32[]{:S(2)}) collective-permute-start(bf16[128,1152]{1,0:T(8,128)(2,1)S(1)} %join.4), channel_id=1, source_target_pairs={{0,64},{1,193},{2,66},{3,195},{4,68},{5,197},{6,70},{7,199},{8,72}... | collective-permute-start | bytes 884744 | tf_op jit(solution)/shard_map/ppermute | solution.py:53
  15.3 22.9 %collective-permute-start.12 = (bf16[256,1152]{1,0:T(8,128)(2,1)S(1)}, bf16[256,1152]{1,0:T(8,128)(2,1)S(1)}, u32[]{:S(2)}, u32[]{:S(2)}) collective-permute-start(bf16[256,1152]{1,0:T(8,128)(2,1)S(1)} %join.3.refs_0_.raw_ref), channel_id=1, source_target_pairs={{0,16},{1,5},{2,18},{3,7},{4,20},{5,1},{6,22},{7,3},{8,24},{9,13},... | collective-permute-start | bytes 1769480 | tf_op jit(solution)/shard_map/ppermute | solution.py:53
  22.0 9.9 %collective-permute-start.5 = (bf16[128,1152]{1,0:T(8,128)(2,1)S(1)}, bf16[128,1152]{1,0:T(8,128)(2,1)S(1)}, u32[]{:S(2)}, u32[]{:S(2)}) collective-permute-start(bf16[128,1152]{1,0:T(8,128)(2,1)S(1)} %collective-permute-done.4.src.refs_3_), channel_id=1, source_target_pairs={{0,32},{1,225},{2,34},{3,227},{4,36},{5,229},{6,38},{7,231},{8,40}... | collective-permute-start | bytes 884744 | tf_op jit(solution)/shard_map/ppermute | solution.py:53
  24.4 8.4 %collective-permute-start.7 = (bf16[128,1152]{1,0:T(8,128)(2,1)S(1)}, bf16[128,1152]{1,0:T(8,128)(2,1)S(1)}, u32[]{:S(2)}, u32[]{:S(2)}) collective-permute-start(bf16[128,1152]{1,0:T(8,128)(2,1)S(1)} %join.4), channel_id=1, source_target_pairs={{0,32},{1,225},{2,34},{3,227},{4,36},{5,229},{6,38},{7,231},{8,40}... | collective-permute-start | bytes 884744 | tf_op jit(solution)/shard_map/ppermute | solution.py:53
  26.6 11.7 %collective-permute-start.11 = (bf16[256,1152]{1,0:T(8,128)(2,1)S(1)}, bf16[256,1152]{1,0:T(8,128)(2,1)S(1)}, u32[]{:S(2)}, u32[]{:S(2)}) collective-permute-start(bf16[256,1152]{1,0:T(8,128)(2,1)S(1)} %join.3.refs_0_.raw_ref), channel_id=1, source_target_pairs={{0,24},{1,7},{2,26},{3,1},{4,28},{5,3},{6,30},{7,5},{8,0},{9,15},{... | collective-permute-start | bytes 1769480 | tf_op jit(solution)/shard_map/ppermute | solution.py:53
  29.1 6.7 %collective-permute-start.6 = (bf16[64,1152]{1,0:T(8,128)(2,1)S(1)}, bf16[64,1152]{1,0:T(8,128)(2,1)S(1)}, u32[]{:S(2)}, u32[]{:S(2)}) collective-permute-start(bf16[64,1152]{1,0:T(8,128)(2,1)S(1)} %head.1), channel_id=1, source_target_pairs={{0,64},{1,193},{2,66},{3,195},{4,68},{5,197},{6,70},{7,199},{8,72}... | collective-permute-start | bytes 442376 | tf_op jit(solution)/shard_map/ppermute | solution.py:53
  31.9 10.3 %collective-permute-start.10 = (bf16[256,1152]{1,0:T(8,128)(2,1)S(1)}, bf16[256,1152]{1,0:T(8,128)(2,1)S(1)}, u32[]{:S(2)}, u32[]{:S(2)}) collective-permute-start(bf16[256,1152]{1,0:T(8,128)(2,1)S(1)} %join.3.refs_0_.raw_ref), channel_id=1, source_target_pairs={{0,8},{1,3},{2,10},{3,5},{4,12},{5,7},{6,14},{7,1},{8,16},{9,11},{... | collective-permute-start | bytes 1769480 | tf_op jit(solution)/shard_map/ppermute | solution.py:53
  32.8 9.6 %collective-permute-start.9 = (s32[8,128]{1,0:T(8,128)S(1)}, s32[8,128]{1,0:T(8,128)S(1)}, u32[]{:S(2)}, u32[]{:S(2)}) collective-permute-start(s32[8,128]{1,0:T(8,128)S(1)} %bitcast.51), channel_id=1, source_target_pairs={{0,16},{1,17},{2,18},{3,19},{4,20},{5,21},{6,22},{7,23},{8,24},{9,... | collective-permute-start | bytes 12296 | tf_op jit(solution)/shard_map/ppermute | solution.py:53
  35.9 7.2 %collective-permute-start.8 = (bf16[448,1152]{1,0:T(8,128)(2,1)S(1)}, bf16[448,1152]{1,0:T(8,128)(2,1)S(1)}, u32[]{:S(2)}, u32[]{:S(2)}) collective-permute-start(bf16[448,1152]{1,0:T(8,128)(2,1)S(1)} %join.5.refs_0_.refs_8_), channel_id=1, source_target_pairs={{0,1},{1,0},{2,3},{3,2},{4,5},{5,4},{6,7},{7,6},{8,9},{9,8},{10,11... | collective-permute-start | bytes 3096584 | tf_op jit(solution)/shard_map/ppermute | solution.py:53
  49.0 5.0 %collective-permute-start.13 = (bf16[192,1152]{1,0:T(8,128)(2,1)S(1)}, bf16[192,1152]{1,0:T(8,128)(2,1)S(1)}, u32[]{:S(2)}, u32[]{:S(2)}) collective-permute-start(bf16[192,1152]{1,0:T(8,128)(2,1)S(1)} %far_give.1), channel_id=1, source_target_pairs={{0,1},{1,0},{2,3},{3,2},{4,5},{5,4},{6,7},{7,6},{8,9},{9,8},{10,11... | collective-permute-start | bytes 1327112 | tf_op jit(solution)/shard_map/ppermute | solution.py:53
  54.1 12.8 %collective-permute-start.15 = (bf16[192,1152]{1,0:T(8,128)(2,1)S(1)}, bf16[192,1152]{1,0:T(8,128)(2,1)S(1)}, u32[]{:S(2)}, u32[]{:S(2)}) collective-permute-start(bf16[192,1152]{1,0:T(8,128)(2,1)S(1)} %add_convert_fusion), channel_id=1, source_target_pairs={{0,64},{1,193},{2,66},{3,195},{4,68},{5,197},{6,70},{7,199},{8,72}... | collective-permute-start | bytes 1327112 | tf_op jit(solution)/shard_map/ppermute | solution.py:53
  56.7 10.2 %collective-permute-start.14 = (bf16[320,1152]{1,0:T(8,128)(2,1)S(1)}, bf16[320,1152]{1,0:T(8,128)(2,1)S(1)}, u32[]{:S(2)}, u32[]{:S(2)}) collective-permute-start(bf16[320,1152]{1,0:T(8,128)(2,1)S(1)} %near_give.1), channel_id=1, source_target_pairs={{0,1},{1,0},{2,3},{3,2},{4,5},{5,4},{6,7},{7,6},{8,9},{9,8},{10,11... | collective-permute-start | bytes 2211848 | tf_op jit(solution)/shard_map/ppermute | solution.py:53
  58.7 16.9 %collective-permute-start.18 = (bf16[256,1152]{1,0:T(8,128)(2,1)S(1)}, bf16[256,1152]{1,0:T(8,128)(2,1)S(1)}, u32[]{:S(2)}, u32[]{:S(2)}) collective-permute-start(bf16[256,1152]{1,0:T(8,128)(2,1)S(1)} %image_sum.5), channel_id=1, source_target_pairs={{0,16},{1,5},{2,18},{3,7},{4,20},{5,1},{6,22},{7,3},{8,24},{9,13},... | collective-permute-start | bytes 1769480 | tf_op jit(solution)/shard_map/ppermute | solution.py:53
  60.1 15.4 %collective-permute-start.17 = (bf16[256,1152]{1,0:T(8,128)(2,1)S(1)}, bf16[256,1152]{1,0:T(8,128)(2,1)S(1)}, u32[]{:S(2)}, u32[]{:S(2)}) collective-permute-start(bf16[256,1152]{1,0:T(8,128)(2,1)S(1)} %image_sum.7), channel_id=1, source_target_pairs={{0,8},{1,3},{2,10},{3,5},{4,12},{5,7},{6,14},{7,1},{8,16},{9,11},{... | collective-permute-start | bytes 1769480 | tf_op jit(solution)/shard_map/ppermute | solution.py:53
  61.7 13.9 %collective-permute-start.16 = (bf16[256,1152]{1,0:T(8,128)(2,1)S(1)}, bf16[256,1152]{1,0:T(8,128)(2,1)S(1)}, u32[]{:S(2)}, u32[]{:S(2)}) collective-permute-start(bf16[256,1152]{1,0:T(8,128)(2,1)S(1)} %image_sum.6), channel_id=1, source_target_pairs={{0,24},{1,7},{2,26},{3,1},{4,28},{5,3},{6,30},{7,5},{8,0},{9,15},{... | collective-permute-start | bytes 1769480 | tf_op jit(solution)/shard_map/ppermute | solution.py:53
  67.3 10.1 %collective-permute-start.23 = (bf16[128,1152]{1,0:T(8,128)(2,1)S(1)}, bf16[128,1152]{1,0:T(8,128)(2,1)S(1)}, u32[]{:S(2)}, u32[]{:S(2)}) collective-permute-start(bf16[128,1152]{1,0:T(8,128)(2,1)S(1)} %pad_maximum_fusion), channel_id=1, source_target_pairs={{0,64},{1,193},{2,66},{3,195},{4,68},{5,197},{6,70},{7,199},{8,72}... | collective-permute-start | bytes 884744 | tf_op jit(solution)/shard_map/ppermute | solution.py:53
  69.7 10.5 %collective-permute-start.22 = (bf16[128,1152]{1,0:T(8,128)(2,1)S(1)}, bf16[128,1152]{1,0:T(8,128)(2,1)S(1)}, u32[]{:S(2)}, u32[]{:S(2)}) collective-permute-start(bf16[128,1152]{1,0:T(8,128)(2,1)S(1)} %slice.46), channel_id=1, source_target_pairs={{0,32},{1,225},{2,34},{3,227},{4,36},{5,229},{6,38},{7,231},{8,40}... | collective-permute-start | bytes 884744 | tf_op jit(solution)/shard_map/ppermute | solution.py:53
  75.9 6.3 %collective-permute-start.19 = (bf16[64,1152]{1,0:T(8,128)(2,1)S(1)}, bf16[64,1152]{1,0:T(8,128)(2,1)S(1)}, u32[]{:S(2)}, u32[]{:S(2)}) collective-permute-start(bf16[64,1152]{1,0:T(8,128)(2,1)S(1)} %get-tuple-element.42), channel_id=1, source_target_pairs={{0,6},{1,25},{2,0},{3,27},{4,2},{5,29},{6,4},{7,31},{8,14},{9,1},{... | collective-permute-start | bytes 442376 | tf_op jit(solution)/shard_map/ppermute | solution.py:53
  76.0 6.3 %collective-permute-start.21 = (bf16[64,1152]{1,0:T(8,128)(2,1)S(1)}, bf16[64,1152]{1,0:T(8,128)(2,1)S(1)}, u32[]{:S(2)}, u32[]{:S(2)}) collective-permute-start(bf16[64,1152]{1,0:T(8,128)(2,1)S(1)} %get-tuple-element.43), channel_id=1, source_target_pairs={{0,4},{1,17},{2,6},{3,19},{4,0},{5,21},{6,2},{7,23},{8,12},{9,25},... | collective-permute-start | bytes 442376 | tf_op jit(solution)/shard_map/ppermute | solution.py:53
  76.2 7.1 %collective-permute-start.20 = (bf16[64,1152]{1,0:T(8,128)(2,1)S(1)}, bf16[64,1152]{1,0:T(8,128)(2,1)S(1)}, u32[]{:S(2)}, u32[]{:S(2)}) collective-permute-start(bf16[64,1152]{1,0:T(8,128)(2,1)S(1)} %get-tuple-element.44), channel_id=1, source_target_pairs={{0,2},{1,9},{2,4},{3,11},{4,6},{5,13},{6,0},{7,15},{8,10},{9,17},{... | collective-permute-start | bytes 442376 | tf_op jit(solution)/shard_map/ppermute | solution.py:53
  (4 other events, 8.6 us)

commit v2 on v1

--- a/solution.py
+++ b/solution.py
@@ -155,7 +155,7 @@
     return jax.ShapeDtypeStruct(shape, dtype)
 
 
-WEIGHT = 0.1
+WEIGHT = 0.15
 
 
 def fast(*arrays):

time: 85.3 us -> 83.9 us (0.984)
  waiting for transfers between devices: 20.8 us -> 16.4 us
  starting transfers between devices: 40.5 us -> 43.8 us
    ppermute x25, waiting for transfers between devices: 20.8 us -> 16.4 us  [send(): return lax.ppermute(v, AXES, perm)]
    ppermute x25, starting transfers between devices: 40.5 us -> 43.8 us  [send(): return lax.ppermute(v, AXES, perm)]
  transfers between devices with their start and end apart: 25 -> 25, of which waited for: 8 -> 9; matrix products, arithmetic and copies ran while one was open for 2% -> 2% of each run, Pallas kernels for 12% -> 12%
where the time goes in v2:
time: 83.9 us; the launch traced here: 83.7 us
  starting transfers between devices  43.8 us (52%)
  waiting for transfers between devices  16.4 us (20%)
  Pallas kernels  15.9 us (19%)
  between operations  3.33 us (4%)
  other arithmetic  2.14 us (3%)
  local copies, waits for them, and re-layouts  2.05 us (2%)
    ppermute x25, starting transfers between devices, send(): return lax.ppermute(v, AXES, perm)  43.8 us
    ppermute x25, waiting for transfers between devices, send(): return lax.ppermute(v, AXES, perm)  16.4 us
    pallas_call x4, Pallas kernels, image_sum(): pl.pallas_call(image_kernel, out_shape=sds(raw.shape, BF16), in_specs=[VM...  4.74 us
    pallas_call x4, Pallas kernels, text_sum(): pl.pallas_call(functools.partial(text_kernel, first, spans), out_shape=sd...  4.55 us
    pallas_call x4, Pallas kernels, tile(): pl.pallas_call(functools.partial(tile_kernel, quarter), out_shape=sds((yh...  4.14 us
    unnamed x6, local copies, waits for them, and re-layouts  1.83 us
  transfers between devices with their start and end apart: 25, of which 9 were waited for; matrix products, arithmetic and copies ran while one was open for 2% of the time, Pallas kernels for 12%

profile of v2, /device:TPU:1, one launch (start us, length us, event | category | flops | bytes accessed | tf_op | source)
XLA Modules:
  0.0 83.7 jit_solution(10043186099341475827)
XLA Ops:
  0.6 3.3 %collective-permute-start.3 = (bf16[64,1152]{1,0:T(8,128)(2,1)}, bf16[64,1152]{1,0:T(8,128)(2,1)S(1)}, u32[]{:S(2)}, u32[]{:S(2)}) collective-permute-start(bf16[64,1152]{1,0:T(8,128)(2,1)} %refs_1_.1), channel_id=1, source_target_pairs={{0,1},{1,0},{2,3},{3,2},{4,5},{5,4},{6,7},{7,6},{8,9},{9,8},{10,11... | collective-permute-start | bytes 442376 | tf_op jit(solution)/shard_map/ppermute | solution.py:53
  4.0 2.2 %collective-permute-start.2 = (bf16[64,1152]{1,0:T(8,128)(2,1)}, bf16[64,1152]{1,0:T(8,128)(2,1)S(1)}, u32[]{:S(2)}, u32[]{:S(2)}) collective-permute-start(bf16[64,1152]{1,0:T(8,128)(2,1)} %refs_0_.1), channel_id=1, source_target_pairs={{0,4},{1,17},{2,6},{3,19},{4,0},{5,21},{6,2},{7,23},{8,12},{9,25},... | collective-permute-start | bytes 442376 | tf_op jit(solution)/shard_map/ppermute | solution.py:53
  9.1 6.1 %collective-permute-start.4 = (bf16[128,1152]{1,0:T(8,128)(2,1)S(1)}, bf16[128,1152]{1,0:T(8,128)(2,1)S(1)}, u32[]{:S(2)}, u32[]{:S(2)}) collective-permute-start(bf16[128,1152]{1,0:T(8,128)(2,1)S(1)} %join.4), channel_id=1, source_target_pairs={{0,64},{1,193},{2,66},{3,195},{4,68},{5,197},{6,70},{7,199},{8,72}... | collective-permute-start | bytes 884744 | tf_op jit(solution)/shard_map/ppermute | solution.py:53
  15.3 2.8 %collective-permute-start.12 = (bf16[256,1152]{1,0:T(8,128)(2,1)S(1)}, bf16[256,1152]{1,0:T(8,128)(2,1)S(1)}, u32[]{:S(2)}, u32[]{:S(2)}) collective-permute-start(bf16[256,1152]{1,0:T(8,128)(2,1)S(1)} %join.3.refs_0_.raw_ref), channel_id=1, source_target_pairs={{0,16},{1,5},{2,18},{3,7},{4,20},{5,1},{6,22},{7,3},{8,24},{9,13},... | collective-permute-start | bytes 1769480 | tf_op jit(solution)/shard_map/ppermute | solution.py:53
  18.1 3.9 %collective-permute-done.4.src.refs_3_ = bf16[128,1152]{1,0:T(8,128)(2,1)S(1)} collective-permute-done((bf16[128,1152]{1,0:T(8,128)(2,1)S(1)}, bf16[128,1152]{1,0:T(8,128)(2,1)S(1)}, u32[]{:S(2)}, u32[]{:S(2)}) %collective-permute-start.4) | collective-permute-done | bytes 294944 | tf_op jit(solution)/shard_map/ppermute | solution.py:53
  22.0 2.4 %collective-permute-start.5 = (bf16[128,1152]{1,0:T(8,128)(2,1)S(1)}, bf16[128,1152]{1,0:T(8,128)(2,1)S(1)}, u32[]{:S(2)}, u32[]{:S(2)}) collective-permute-start(bf16[128,1152]{1,0:T(8,128)(2,1)S(1)} %collective-permute-done.4.src.refs_3_), channel_id=1, source_target_pairs={{0,32},{1,225},{2,34},{3,227},{4,36},{5,229},{6,38},{7,231},{8,40}... | collective-permute-start | bytes 884744 | tf_op jit(solution)/shard_map/ppermute | solution.py:53
  24.4 2.2 %collective-permute-start.7 = (bf16[128,1152]{1,0:T(8,128)(2,1)S(1)}, bf16[128,1152]{1,0:T(8,128)(2,1)S(1)}, u32[]{:S(2)}, u32[]{:S(2)}) collective-permute-start(bf16[128,1152]{1,0:T(8,128)(2,1)S(1)} %join.4), channel_id=1, source_target_pairs={{0,32},{1,225},{2,34},{3,227},{4,36},{5,229},{6,38},{7,231},{8,40}... | collective-permute-start | bytes 884744 | tf_op jit(solution)/shard_map/ppermute | solution.py:53
  29.2 2.6 %collective-permute-start.11 = (bf16[256,1152]{1,0:T(8,128)(2,1)S(1)}, bf16[256,1152]{1,0:T(8,128)(2,1)S(1)}, u32[]{:S(2)}, u32[]{:S(2)}) collective-permute-start(bf16[256,1152]{1,0:T(8,128)(2,1)S(1)} %join.3.refs_0_.raw_ref), channel_id=1, source_target_pairs={{0,24},{1,7},{2,26},{3,1},{4,28},{5,3},{6,30},{7,5},{8,0},{9,15},{... | collective-permute-start | bytes 1769480 | tf_op jit(solution)/shard_map/ppermute | solution.py:53
  32.1 1.6 %collective-permute-start.9 = (s32[8,128]{1,0:T(8,128)S(1)}, s32[8,128]{1,0:T(8,128)S(1)}, u32[]{:S(2)}, u32[]{:S(2)}) collective-permute-start(s32[8,128]{1,0:T(8,128)S(1)} %bitcast.51), channel_id=1, source_target_pairs={{0,16},{1,17},{2,18},{3,19},{4,20},{5,21},{6,22},{7,23},{8,24},{9,... | collective-permute-start | bytes 12296 | tf_op jit(solution)/shard_map/ppermute | solution.py:53
  34.5 3.6 %collective-permute-start.8 = (bf16[448,1152]{1,0:T(8,128)(2,1)S(1)}, bf16[448,1152]{1,0:T(8,128)(2,1)S(1)}, u32[]{:S(2)}, u32[]{:S(2)}) collective-permute-start(bf16[448,1152]{1,0:T(8,128)(2,1)S(1)} %join.5.refs_0_.refs_8_), channel_id=1, source_target_pairs={{0,1},{1,0},{2,3},{3,2},{4,5},{5,4},{6,7},{7,6},{8,9},{9,8},{10,11... | collective-permute-start | bytes 3096584 | tf_op jit(solution)/shard_map/ppermute | solution.py:53
  38.8 3.5 %collective-permute-done.10.refs_0_.raw_ref = bf16[256,1152]{1,0:T(8,128)(2,1)S(1)} collective-permute-done((bf16[256,1152]{1,0:T(8,128)(2,1)S(1)}, bf16[256,1152]{1,0:T(8,128)(2,1)S(1)}, u32[]{:S(2)}, u32[]{:S(2)}) %collective-permute-start.10) | collective-permute-done | bytes 589856 | tf_op jit(solution)/shard_map/ppermute | solution.py:53
  49.1 3.5 %collective-permute-start.13 = (bf16[192,1152]{1,0:T(8,128)(2,1)S(1)}, bf16[192,1152]{1,0:T(8,128)(2,1)S(1)}, u32[]{:S(2)}, u32[]{:S(2)}) collective-permute-start(bf16[192,1152]{1,0:T(8,128)(2,1)S(1)} %far_give.1), channel_id=1, source_target_pairs={{0,1},{1,0},{2,3},{3,2},{4,5},{5,4},{6,7},{7,6},{8,9},{9,8},{10,11... | collective-permute-start | bytes 1327112 | tf_op jit(solution)/shard_map/ppermute | solution.py:53
  54.2 1.2 %image_sum.5 = bf16[256,1152]{1,0:T(8,128)(2,1)S(1)} custom-call(bf16[256,1152]{1,0:T(8,128)(2,1)S(1)} %collective-permute-done.12.refs_0_.raw_ref, bf16[1024,1152]{1,0:T(8,128)(2,1)S(1)} %normalize.5.yh_ref, bf16[1024,256]{1,0:T(8,128)(2,1)S(1)} %tile.7.refs_3_.g_ref), custom_call_target="tpu_custom_call" | custom-call | flops 276000000 | bytes 1 | tf_op jit(solution)/shard_map/image_sum/pallas_call | solution.py:256
  55.8 1.4 %near_give.1 = bf16[320,1152]{1,0:T(8,128)(2,1)S(1)} custom-call(bf16[1024,256]{1,0:T(8,128)(2,1)S(1)} %tile.4.refs_0_.g_ref, bf16[1024,256]{1,0:T(8,128)(2,1)S(1)} %tile.5.refs_1_.g_ref, bf16[1024,256]{1,0:T(8,128)(2,1)S(1)} %tile.6.refs_2_.g_ref, bf16[1024,256]{1,0:T(8,128)(2,1)S(1)} %tile.7.refs_3_.g_ref, bf16[256,1152]{1,0:T(8,128)(2,1)S(1)} %normalize.6.xh_ref.refs_4_, ...), custom_call_target="tpu_custom_call" | custom-call | flops 240000000 | bytes 1 | tf_op jit(solution)/shard_map/near_give/pallas_call | solution.py:273
  57.1 1.8 %collective-permute-start.14 = (bf16[320,1152]{1,0:T(8,128)(2,1)S(1)}, bf16[320,1152]{1,0:T(8,128)(2,1)S(1)}, u32[]{:S(2)}, u32[]{:S(2)}) collective-permute-start(bf16[320,1152]{1,0:T(8,128)(2,1)S(1)} %near_give.1), channel_id=1, source_target_pairs={{0,1},{1,0},{2,3},{3,2},{4,5},{5,4},{6,7},{7,6},{8,9},{9,8},{10,11... | collective-permute-start | bytes 2211848 | tf_op jit(solution)/shard_map/ppermute | solution.py:53
  58.9 1.2 %image_sum.7 = bf16[256,1152]{1,0:T(8,128)(2,1)S(1)} custom-call(bf16[256,1152]{1,0:T(8,128)(2,1)S(1)} %collective-permute-done.11.refs_0_.raw_ref, bf16[1024,1152]{1,0:T(8,128)(2,1)S(1)} %normalize.5.yh_ref, bf16[1024,256]{1,0:T(8,128)(2,1)S(1)} %tile.6.refs_2_.g_ref), custom_call_target="tpu_custom_call" | custom-call | flops 276000000 | bytes 1 | tf_op jit(solution)/shard_map/image_sum/pallas_call | solution.py:256
  61.9 2.5 %collective-permute-start.16 = (bf16[256,1152]{1,0:T(8,128)(2,1)S(1)}, bf16[256,1152]{1,0:T(8,128)(2,1)S(1)}, u32[]{:S(2)}, u32[]{:S(2)}) collective-permute-start(bf16[256,1152]{1,0:T(8,128)(2,1)S(1)} %image_sum.6), channel_id=1, source_target_pairs={{0,24},{1,7},{2,26},{3,1},{4,28},{5,3},{6,30},{7,5},{8,0},{9,15},{... | collective-permute-start | bytes 1769480 | tf_op jit(solution)/shard_map/ppermute | solution.py:53
  64.4 1.4 %near_keep.1 = bf16[320,1152]{1,0:T(8,128)(2,1)S(1)} custom-call(bf16[1024,256]{1,0:T(8,128)(2,1)S(1)} %tile.4.refs_0_.g_ref, bf16[1024,256]{1,0:T(8,128)(2,1)S(1)} %tile.5.refs_1_.g_ref, bf16[1024,256]{1,0:T(8,128)(2,1)S(1)} %tile.6.refs_2_.g_ref, bf16[1024,256]{1,0:T(8,128)(2,1)S(1)} %tile.7.refs_3_.g_ref, bf16[256,1152]{1,0:T(8,128)(2,1)S(1)} %normalize.6.xh_ref.refs_4_, ...), custom_call_target="tpu_custom_call" | custom-call | flops 240000000 | bytes 1 | tf_op jit(solution)/shard_map/near_keep/pallas_call | solution.py:273
  67.3 2.4 %collective-permute-start.23 = (bf16[128,1152]{1,0:T(8,128)(2,1)S(1)}, bf16[128,1152]{1,0:T(8,128)(2,1)S(1)}, u32[]{:S(2)}, u32[]{:S(2)}) collective-permute-start(bf16[128,1152]{1,0:T(8,128)(2,1)S(1)} %pad_maximum_fusion), channel_id=1, source_target_pairs={{0,64},{1,193},{2,66},{3,195},{4,68},{5,197},{6,70},{7,199},{8,72}... | collective-permute-start | bytes 884744 | tf_op jit(solution)/shard_map/ppermute | solution.py:53
  69.8 2.6 %collective-permute-done.17 = bf16[256,1152]{1,0:T(8,128)(2,1)S(1)} collective-permute-done((bf16[256,1152]{1,0:T(8,128)(2,1)S(1)}, bf16[256,1152]{1,0:T(8,128)(2,1)S(1)}, u32[]{:S(2)}, u32[]{:S(2)}) %collective-permute-start.17) | collective-permute-done | bytes 589856 | tf_op jit(solution)/shard_map/ppermute | solution.py:53
  73.2 1.7 %collective-permute-start.21 = (bf16[64,1152]{1,0:T(8,128)(2,1)S(1)}, bf16[64,1152]{1,0:T(8,128)(2,1)S(1)}, u32[]{:S(2)}, u32[]{:S(2)}) collective-permute-start(bf16[64,1152]{1,0:T(8,128)(2,1)S(1)} %get-tuple-element.43), channel_id=1, source_target_pairs={{0,4},{1,17},{2,6},{3,19},{4,0},{5,21},{6,2},{7,23},{8,12},{9,25},... | collective-permute-start | bytes 442376 | tf_op jit(solution)/shard_map/ppermute | solution.py:53
  75.6 1.7 %collective-permute-done.23.refs_1_ = bf16[128,1152]{1,0:T(8,128)(2,1)S(1)} collective-permute-done((bf16[128,1152]{1,0:T(8,128)(2,1)S(1)}, bf16[128,1152]{1,0:T(8,128)(2,1)S(1)}, u32[]{:S(2)}, u32[]{:S(2)}) %collective-permute-start.23) | collective-permute-done | bytes 294944 | tf_op jit(solution)/shard_map/ppermute | solution.py:53
  77.4 2.9 %collective-permute-done.22.refs_0_ = bf16[128,1152]{1,0:T(8,128)(2,1)S(1)} collective-permute-done((bf16[128,1152]{1,0:T(8,128)(2,1)S(1)}, bf16[128,1152]{1,0:T(8,128)(2,1)S(1)}, u32[]{:S(2)}, u32[]{:S(2)}) %collective-permute-start.22) | collective-permute-done | bytes 294944 | tf_op jit(solution)/shard_map/ppermute | solution.py:53
  80.3 1.6 %collective-permute-start.24 = (bf16[64,1152]{1,0:T(8,128)(2,1)S(1)}, bf16[64,1152]{1,0:T(8,128)(2,1)S(1)}, u32[]{:S(2)}, u32[]{:S(2)}) collective-permute-start(bf16[64,1152]{1,0:T(8,128)(2,1)S(1)} %add_convert_fusion.1), channel_id=1, source_target_pairs={{0,1},{1,0},{2,3},{3,2},{4,5},{5,4},{6,7},{7,6},{8,9},{9,8},{10,11... | collective-permute-start | bytes 442376 | tf_op jit(solution)/shard_map/ppermute | solution.py:53
  (70 shorter events, 20.3 us)
Async XLA Ops:
  0.6 8.4 %collective-permute-start.3 = (bf16[64,1152]{1,0:T(8,128)(2,1)}, bf16[64,1152]{1,0:T(8,128)(2,1)S(1)}, u32[]{:S(2)}, u32[]{:S(2)}) collective-permute-start(bf16[64,1152]{1,0:T(8,128)(2,1)} %refs_1_.1), channel_id=1, source_target_pairs={{0,1},{1,0},{2,3},{3,2},{4,5},{5,4},{6,7},{7,6},{8,9},{9,8},{10,11... | collective-permute-start | bytes 442376 | tf_op jit(solution)/shard_map/ppermute | solution.py:53
  4.0 11.2 %collective-permute-start = (bf16[64,1152]{1,0:T(8,128)(2,1)}, bf16[64,1152]{1,0:T(8,128)(2,1)S(1)}, u32[]{:S(2)}, u32[]{:S(2)}) collective-permute-start(bf16[64,1152]{1,0:T(8,128)(2,1)} %refs_0_.1), channel_id=1, source_target_pairs={{0,2},{1,9},{2,4},{3,11},{4,6},{5,13},{6,0},{7,15},{8,10},{9,17},{... | collective-permute-start | bytes 442376 | tf_op jit(solution)/shard_map/ppermute | solution.py:53
  4.0 11.2 %collective-permute-start.2 = (bf16[64,1152]{1,0:T(8,128)(2,1)}, bf16[64,1152]{1,0:T(8,128)(2,1)S(1)}, u32[]{:S(2)}, u32[]{:S(2)}) collective-permute-start(bf16[64,1152]{1,0:T(8,128)(2,1)} %refs_0_.1), channel_id=1, source_target_pairs={{0,4},{1,17},{2,6},{3,19},{4,0},{5,21},{6,2},{7,23},{8,12},{9,25},... | collective-permute-start | bytes 442376 | tf_op jit(solution)/shard_map/ppermute | solution.py:53
  6.1 9.1 %collective-permute-start.1 = (bf16[64,1152]{1,0:T(8,128)(2,1)}, bf16[64,1152]{1,0:T(8,128)(2,1)S(1)}, u32[]{:S(2)}, u32[]{:S(2)}) collective-permute-start(bf16[64,1152]{1,0:T(8,128)(2,1)} %refs_0_.1), channel_id=1, source_target_pairs={{0,6},{1,25},{2,0},{3,27},{4,2},{5,29},{6,4},{7,31},{8,14},{9,1},{... | collective-permute-start | bytes 442376 | tf_op jit(solution)/shard_map/ppermute | solution.py:53
  9.1 12.9 %collective-permute-start.4 = (bf16[128,1152]{1,0:T(8,128)(2,1)S(1)}, bf16[128,1152]{1,0:T(8,128)(2,1)S(1)}, u32[]{:S(2)}, u32[]{:S(2)}) collective-permute-start(bf16[128,1152]{1,0:T(8,128)(2,1)S(1)} %join.4), channel_id=1, source_target_pairs={{0,64},{1,193},{2,66},{3,195},{4,68},{5,197},{6,70},{7,199},{8,72}... | collective-permute-start | bytes 884744 | tf_op jit(solution)/shard_map/ppermute | solution.py:53
  15.3 22.9 %collective-permute-start.12 = (bf16[256,1152]{1,0:T(8,128)(2,1)S(1)}, bf16[256,1152]{1,0:T(8,128)(2,1)S(1)}, u32[]{:S(2)}, u32[]{:S(2)}) collective-permute-start(bf16[256,1152]{1,0:T(8,128)(2,1)S(1)} %join.3.refs_0_.raw_ref), channel_id=1, source_target_pairs={{0,16},{1,5},{2,18},{3,7},{4,20},{5,1},{6,22},{7,3},{8,24},{9,13},... | collective-permute-start | bytes 1769480 | tf_op jit(solution)/shard_map/ppermute | solution.py:53
  22.0 10.0 %collective-permute-start.5 = (bf16[128,1152]{1,0:T(8,128)(2,1)S(1)}, bf16[128,1152]{1,0:T(8,128)(2,1)S(1)}, u32[]{:S(2)}, u32[]{:S(2)}) collective-permute-start(bf16[128,1152]{1,0:T(8,128)(2,1)S(1)} %collective-permute-done.4.src.refs_3_), channel_id=1, source_target_pairs={{0,32},{1,225},{2,34},{3,227},{4,36},{5,229},{6,38},{7,231},{8,40}... | collective-permute-start | bytes 884744 | tf_op jit(solution)/shard_map/ppermute | solution.py:53
  24.4 7.6 %collective-permute-start.7 = (bf16[128,1152]{1,0:T(8,128)(2,1)S(1)}, bf16[128,1152]{1,0:T(8,128)(2,1)S(1)}, u32[]{:S(2)}, u32[]{:S(2)}) collective-permute-start(bf16[128,1152]{1,0:T(8,128)(2,1)S(1)} %join.4), channel_id=1, source_target_pairs={{0,32},{1,225},{2,34},{3,227},{4,36},{5,229},{6,38},{7,231},{8,40}... | collective-permute-start | bytes 884744 | tf_op jit(solution)/shard_map/ppermute | solution.py:53
  26.6 7.8 %collective-permute-start.6 = (bf16[64,1152]{1,0:T(8,128)(2,1)S(1)}, bf16[64,1152]{1,0:T(8,128)(2,1)S(1)}, u32[]{:S(2)}, u32[]{:S(2)}) collective-permute-start(bf16[64,1152]{1,0:T(8,128)(2,1)S(1)} %head.1), channel_id=1, source_target_pairs={{0,64},{1,193},{2,66},{3,195},{4,68},{5,197},{6,70},{7,199},{8,72}... | collective-permute-start | bytes 442376 | tf_op jit(solution)/shard_map/ppermute | solution.py:53
  29.2 9.4 %collective-permute-start.11 = (bf16[256,1152]{1,0:T(8,128)(2,1)S(1)}, bf16[256,1152]{1,0:T(8,128)(2,1)S(1)}, u32[]{:S(2)}, u32[]{:S(2)}) collective-permute-start(bf16[256,1152]{1,0:T(8,128)(2,1)S(1)} %join.3.refs_0_.raw_ref), channel_id=1, source_target_pairs={{0,24},{1,7},{2,26},{3,1},{4,28},{5,3},{6,30},{7,5},{8,0},{9,15},{... | collective-permute-start | bytes 1769480 | tf_op jit(solution)/shard_map/ppermute | solution.py:53
  32.0 10.3 %collective-permute-start.10 = (bf16[256,1152]{1,0:T(8,128)(2,1)S(1)}, bf16[256,1152]{1,0:T(8,128)(2,1)S(1)}, u32[]{:S(2)}, u32[]{:S(2)}) collective-permute-start(bf16[256,1152]{1,0:T(8,128)(2,1)S(1)} %join.3.refs_0_.raw_ref), channel_id=1, source_target_pairs={{0,8},{1,3},{2,10},{3,5},{4,12},{5,7},{6,14},{7,1},{8,16},{9,11},{... | collective-permute-start | bytes 1769480 | tf_op jit(solution)/shard_map/ppermute | solution.py:53
  32.1 10.4 %collective-permute-start.9 = (s32[8,128]{1,0:T(8,128)S(1)}, s32[8,128]{1,0:T(8,128)S(1)}, u32[]{:S(2)}, u32[]{:S(2)}) collective-permute-start(s32[8,128]{1,0:T(8,128)S(1)} %bitcast.51), channel_id=1, source_target_pairs={{0,16},{1,17},{2,18},{3,19},{4,20},{5,21},{6,22},{7,23},{8,24},{9,... | collective-permute-start | bytes 12296 | tf_op jit(solution)/shard_map/ppermute | solution.py:53
  34.5 8.7 %collective-permute-start.8 = (bf16[448,1152]{1,0:T(8,128)(2,1)S(1)}, bf16[448,1152]{1,0:T(8,128)(2,1)S(1)}, u32[]{:S(2)}, u32[]{:S(2)}) collective-permute-start(bf16[448,1152]{1,0:T(8,128)(2,1)S(1)} %join.5.refs_0_.refs_8_), channel_id=1, source_target_pairs={{0,1},{1,0},{2,3},{3,2},{4,5},{5,4},{6,7},{7,6},{8,9},{9,8},{10,11... | collective-permute-start | bytes 3096584 | tf_op jit(solution)/shard_map/ppermute | solution.py:53
  49.1 5.0 %collective-permute-start.13 = (bf16[192,1152]{1,0:T(8,128)(2,1)S(1)}, bf16[192,1152]{1,0:T(8,128)(2,1)S(1)}, u32[]{:S(2)}, u32[]{:S(2)}) collective-permute-start(bf16[192,1152]{1,0:T(8,128)(2,1)S(1)} %far_give.1), channel_id=1, source_target_pairs={{0,1},{1,0},{2,3},{3,2},{4,5},{5,4},{6,7},{7,6},{8,9},{9,8},{10,11... | collective-permute-start | bytes 1327112 | tf_op jit(solution)/shard_map/ppermute | solution.py:53
  54.1 12.8 %collective-permute-start.15 = (bf16[192,1152]{1,0:T(8,128)(2,1)S(1)}, bf16[192,1152]{1,0:T(8,128)(2,1)S(1)}, u32[]{:S(2)}, u32[]{:S(2)}) collective-permute-start(bf16[192,1152]{1,0:T(8,128)(2,1)S(1)} %add_convert_fusion), channel_id=1, source_target_pairs={{0,64},{1,193},{2,66},{3,195},{4,68},{5,197},{6,70},{7,199},{8,72}... | collective-permute-start | bytes 1327112 | tf_op jit(solution)/shard_map/ppermute | solution.py:53
  55.4 16.9 %collective-permute-start.18 = (bf16[256,1152]{1,0:T(8,128)(2,1)S(1)}, bf16[256,1152]{1,0:T(8,128)(2,1)S(1)}, u32[]{:S(2)}, u32[]{:S(2)}) collective-permute-start(bf16[256,1152]{1,0:T(8,128)(2,1)S(1)} %image_sum.5), channel_id=1, source_target_pairs={{0,16},{1,5},{2,18},{3,7},{4,20},{5,1},{6,22},{7,3},{8,24},{9,13},... | collective-permute-start | bytes 1769480 | tf_op jit(solution)/shard_map/ppermute | solution.py:53
  57.1 9.8 %collective-permute-start.14 = (bf16[320,1152]{1,0:T(8,128)(2,1)S(1)}, bf16[320,1152]{1,0:T(8,128)(2,1)S(1)}, u32[]{:S(2)}, u32[]{:S(2)}) collective-permute-start(bf16[320,1152]{1,0:T(8,128)(2,1)S(1)} %near_give.1), channel_id=1, source_target_pairs={{0,1},{1,0},{2,3},{3,2},{4,5},{5,4},{6,7},{7,6},{8,9},{9,8},{10,11... | collective-permute-start | bytes 2211848 | tf_op jit(solution)/shard_map/ppermute | solution.py:53
  60.1 12.3 %collective-permute-start.17 = (bf16[256,1152]{1,0:T(8,128)(2,1)S(1)}, bf16[256,1152]{1,0:T(8,128)(2,1)S(1)}, u32[]{:S(2)}, u32[]{:S(2)}) collective-permute-start(bf16[256,1152]{1,0:T(8,128)(2,1)S(1)} %image_sum.7), channel_id=1, source_target_pairs={{0,8},{1,3},{2,10},{3,5},{4,12},{5,7},{6,14},{7,1},{8,16},{9,11},{... | collective-permute-start | bytes 1769480 | tf_op jit(solution)/shard_map/ppermute | solution.py:53
  61.9 10.5 %collective-permute-start.16 = (bf16[256,1152]{1,0:T(8,128)(2,1)S(1)}, bf16[256,1152]{1,0:T(8,128)(2,1)S(1)}, u32[]{:S(2)}, u32[]{:S(2)}) collective-permute-start(bf16[256,1152]{1,0:T(8,128)(2,1)S(1)} %image_sum.6), channel_id=1, source_target_pairs={{0,24},{1,7},{2,26},{3,1},{4,28},{5,3},{6,30},{7,5},{8,0},{9,15},{... | collective-permute-start | bytes 1769480 | tf_op jit(solution)/shard_map/ppermute | solution.py:53
  67.3 10.0 %collective-permute-start.23 = (bf16[128,1152]{1,0:T(8,128)(2,1)S(1)}, bf16[128,1152]{1,0:T(8,128)(2,1)S(1)}, u32[]{:S(2)}, u32[]{:S(2)}) collective-permute-start(bf16[128,1152]{1,0:T(8,128)(2,1)S(1)} %pad_maximum_fusion), channel_id=1, source_target_pairs={{0,64},{1,193},{2,66},{3,195},{4,68},{5,197},{6,70},{7,199},{8,72}... | collective-permute-start | bytes 884744 | tf_op jit(solution)/shard_map/ppermute | solution.py:53
  69.8 10.5 %collective-permute-start.22 = (bf16[128,1152]{1,0:T(8,128)(2,1)S(1)}, bf16[128,1152]{1,0:T(8,128)(2,1)S(1)}, u32[]{:S(2)}, u32[]{:S(2)}) collective-permute-start(bf16[128,1152]{1,0:T(8,128)(2,1)S(1)} %slice.46), channel_id=1, source_target_pairs={{0,32},{1,225},{2,34},{3,227},{4,36},{5,229},{6,38},{7,231},{8,40}... | collective-permute-start | bytes 884744 | tf_op jit(solution)/shard_map/ppermute | solution.py:53
  72.7 9.3 %collective-permute-start.19 = (bf16[64,1152]{1,0:T(8,128)(2,1)S(1)}, bf16[64,1152]{1,0:T(8,128)(2,1)S(1)}, u32[]{:S(2)}, u32[]{:S(2)}) collective-permute-start(bf16[64,1152]{1,0:T(8,128)(2,1)S(1)} %get-tuple-element.42), channel_id=1, source_target_pairs={{0,6},{1,25},{2,0},{3,27},{4,2},{5,29},{6,4},{7,31},{8,14},{9,1},{... | collective-permute-start | bytes 442376 | tf_op jit(solution)/shard_map/ppermute | solution.py:53
  73.2 8.8 %collective-permute-start.21 = (bf16[64,1152]{1,0:T(8,128)(2,1)S(1)}, bf16[64,1152]{1,0:T(8,128)(2,1)S(1)}, u32[]{:S(2)}, u32[]{:S(2)}) collective-permute-start(bf16[64,1152]{1,0:T(8,128)(2,1)S(1)} %get-tuple-element.43), channel_id=1, source_target_pairs={{0,4},{1,17},{2,6},{3,19},{4,0},{5,21},{6,2},{7,23},{8,12},{9,25},... | collective-permute-start | bytes 442376 | tf_op jit(solution)/shard_map/ppermute | solution.py:53
  74.9 7.1 %collective-permute-start.20 = (bf16[64,1152]{1,0:T(8,128)(2,1)S(1)}, bf16[64,1152]{1,0:T(8,128)(2,1)S(1)}, u32[]{:S(2)}, u32[]{:S(2)}) collective-permute-start(bf16[64,1152]{1,0:T(8,128)(2,1)S(1)} %get-tuple-element.44), channel_id=1, source_target_pairs={{0,2},{1,9},{2,4},{3,11},{4,6},{5,13},{6,0},{7,15},{8,10},{9,17},{... | collective-permute-start | bytes 442376 | tf_op jit(solution)/shard_map/ppermute | solution.py:53
  (4 other events, 9.3 us)

commit v3 on v2

--- a/solution.py
+++ b/solution.py
@@ -214,6 +214,24 @@
     )(*fast(array))
 
 
+def norm_each_kernel(*refs):
+    half = len(refs) // 2
+    for src, dst in zip(refs[:half], refs[half:]):
+        norm_kernel(src, dst)
+
+
+def normalize_each(*arrays, us=0.6):
+    return pl.pallas_call(
+        norm_each_kernel,
+        out_shape=tuple(sds(a.shape, BF16) for a in arrays),
+        in_specs=[VM] * len(arrays),
+        out_specs=tuple([VM] * len(arrays)),
+        compiler_params=PARAMS,
+        cost_estimate=cost(us),
+        name="normalize_each",
+    )(*fast(*arrays))
+
+
 def normalize(*pieces, us=0.8):
     rows = sum(p.shape[0] for p in pieces)
     width = pieces[0].shape[1]
@@ -334,10 +352,16 @@
 
     row = join(images, send(image_emb, A_ON), send(image_emb, A_BACK), send(image_emb, A_TWO))
     quarters = [row, send(row, B_ON), send(row, B_BACK), send(row, B_TWO)]
-    xs = [normalize(quarters[0], us=0.3)] + [normalize(q, us=40) for q in quarters[1:]]
 
     yh_all = normalize(give, other, keep, text_emb)
-    gs = [tile(k, weight, pos, ids, xs[k], yh_all) for k in range(4)]
+    xs, gs = [None] * 4, [None] * 4
+    xs[0] = normalize(quarters[0], us=0.3)
+    xs[2], xs[3] = normalize_each(quarters[2], quarters[3], us=100)
+    for k in (0, 2, 3):
+        gs[k] = tile(k, weight, pos, ids, xs[k], yh_all)
+    quarters[1], gs[0], gs[2], gs[3] = lax.optimization_barrier((quarters[1], gs[0], gs[2], gs[3]))
+    xs[1] = normalize(quarters[1], us=20)
+    gs[1] = tile(1, weight, pos, ids, xs[1], yh_all)
     d_give = text_sum(0, gs, xs, far_give, "far_give")
     swapped = send(d_give, CORE)
     d_keep = text_sum(512, gs, xs, far_keep, "far_keep")

time: 83.9 us -> 84 us (level)
  transfers between devices with their start and end apart: 25 -> 25, of which waited for: 9 -> 9; matrix products, arithmetic and copies ran while one was open for 2% -> 2% of each run, Pallas kernels for 12% -> 16%
where the time goes in v3:
time: 84 us; the launch traced here: 83.8 us
  starting transfers between devices  44.5 us (53%)
  Pallas kernels  15.9 us (19%)
  waiting for transfers between devices  15.8 us (19%)
  between operations  3.31 us (4%)
  other arithmetic  2.15 us (3%)
  local copies, waits for them, and re-layouts  2.05 us (2%)
    ppermute x25, starting transfers between devices, send(): return lax.ppermute(v, AXES, perm)  44.5 us
    ppermute x25, waiting for transfers between devices, send(): return lax.ppermute(v, AXES, perm)  15.8 us
    pallas_call x4, Pallas kernels, image_sum(): pl.pallas_call(image_kernel, out_shape=sds(raw.shape, BF16), in_specs=[VM...  4.74 us
    pallas_call x4, Pallas kernels, text_sum(): pl.pallas_call(functools.partial(text_kernel, first, spans), out_shape=sd...  4.55 us
    pallas_call x4, Pallas kernels, tile(): pl.pallas_call(functools.partial(tile_kernel, quarter), out_shape=sds((yh...  4.14 us
    unnamed x6, local copies, waits for them, and re-layouts  1.83 us
  transfers between devices with their start and end apart: 25, of which 9 were waited for; matrix products, arithmetic and copies ran while one was open for 2% of the time, Pallas kernels for 16%

profile of v3, /device:TPU:1, one launch (start us, length us, event | category | flops | bytes accessed | tf_op | source)
XLA Modules:
  0.0 83.8 jit_solution(9165756549367266770)
XLA Ops:
  0.6 3.3 %collective-permute-start.3 = (bf16[64,1152]{1,0:T(8,128)(2,1)}, bf16[64,1152]{1,0:T(8,128)(2,1)S(1)}, u32[]{:S(2)}, u32[]{:S(2)}) collective-permute-start(bf16[64,1152]{1,0:T(8,128)(2,1)} %refs_1_.1), channel_id=1, source_target_pairs={{0,1},{1,0},{2,3},{3,2},{4,5},{5,4},{6,7},{7,6},{8,9},{9,8},{10,11... | collective-permute-start | bytes 442376 | tf_op jit(solution)/shard_map/ppermute | solution.py:53
  4.0 2.2 %collective-permute-start.2 = (bf16[64,1152]{1,0:T(8,128)(2,1)}, bf16[64,1152]{1,0:T(8,128)(2,1)S(1)}, u32[]{:S(2)}, u32[]{:S(2)}) collective-permute-start(bf16[64,1152]{1,0:T(8,128)(2,1)} %refs_0_.1), channel_id=1, source_target_pairs={{0,4},{1,17},{2,6},{3,19},{4,0},{5,21},{6,2},{7,23},{8,12},{9,25},... | collective-permute-start | bytes 442376 | tf_op jit(solution)/shard_map/ppermute | solution.py:53
  9.1 6.1 %collective-permute-start.4 = (bf16[128,1152]{1,0:T(8,128)(2,1)S(1)}, bf16[128,1152]{1,0:T(8,128)(2,1)S(1)}, u32[]{:S(2)}, u32[]{:S(2)}) collective-permute-start(bf16[128,1152]{1,0:T(8,128)(2,1)S(1)} %join.4), channel_id=1, source_target_pairs={{0,64},{1,193},{2,66},{3,195},{4,68},{5,197},{6,70},{7,199},{8,72}... | collective-permute-start | bytes 884744 | tf_op jit(solution)/shard_map/ppermute | solution.py:53
  15.3 2.8 %collective-permute-start.12 = (bf16[256,1152]{1,0:T(8,128)(2,1)S(1)}, bf16[256,1152]{1,0:T(8,128)(2,1)S(1)}, u32[]{:S(2)}, u32[]{:S(2)}) collective-permute-start(bf16[256,1152]{1,0:T(8,128)(2,1)S(1)} %join.3.refs_0_.raw_ref), channel_id=1, source_target_pairs={{0,16},{1,5},{2,18},{3,7},{4,20},{5,1},{6,22},{7,3},{8,24},{9,13},... | collective-permute-start | bytes 1769480 | tf_op jit(solution)/shard_map/ppermute | solution.py:53
  19.0 3.1 %collective-permute-done.4.src.refs_3_ = bf16[128,1152]{1,0:T(8,128)(2,1)S(1)} collective-permute-done((bf16[128,1152]{1,0:T(8,128)(2,1)S(1)}, bf16[128,1152]{1,0:T(8,128)(2,1)S(1)}, u32[]{:S(2)}, u32[]{:S(2)}) %collective-permute-start.4) | collective-permute-done | bytes 294944 | tf_op jit(solution)/shard_map/ppermute | solution.py:53
  22.0 2.4 %collective-permute-start.5 = (bf16[128,1152]{1,0:T(8,128)(2,1)S(1)}, bf16[128,1152]{1,0:T(8,128)(2,1)S(1)}, u32[]{:S(2)}, u32[]{:S(2)}) collective-permute-start(bf16[128,1152]{1,0:T(8,128)(2,1)S(1)} %collective-permute-done.4.src.refs_3_), channel_id=1, source_target_pairs={{0,32},{1,225},{2,34},{3,227},{4,36},{5,229},{6,38},{7,231},{8,40}... | collective-permute-start | bytes 884744 | tf_op jit(solution)/shard_map/ppermute | solution.py:53
  24.4 2.2 %collective-permute-start.7 = (bf16[128,1152]{1,0:T(8,128)(2,1)S(1)}, bf16[128,1152]{1,0:T(8,128)(2,1)S(1)}, u32[]{:S(2)}, u32[]{:S(2)}) collective-permute-start(bf16[128,1152]{1,0:T(8,128)(2,1)S(1)} %join.4), channel_id=1, source_target_pairs={{0,32},{1,225},{2,34},{3,227},{4,36},{5,229},{6,38},{7,231},{8,40}... | collective-permute-start | bytes 884744 | tf_op jit(solution)/shard_map/ppermute | solution.py:53
  29.4 1.3 %collective-permute-start.9 = (bf16[256,1152]{1,0:T(8,128)(2,1)S(1)}, bf16[256,1152]{1,0:T(8,128)(2,1)S(1)}, u32[]{:S(2)}, u32[]{:S(2)}) collective-permute-start(bf16[256,1152]{1,0:T(8,128)(2,1)S(1)} %join.3.refs_0_.raw_ref), channel_id=1, source_target_pairs={{0,8},{1,3},{2,10},{3,5},{4,12},{5,7},{6,14},{7,1},{8,16},{9,11},{... | collective-permute-start | bytes 1769480 | tf_op jit(solution)/shard_map/ppermute | solution.py:53
  31.8 1.9 %collective-permute-start.10 = (s32[8,128]{1,0:T(8,128)S(1)}, s32[8,128]{1,0:T(8,128)S(1)}, u32[]{:S(2)}, u32[]{:S(2)}) collective-permute-start(s32[8,128]{1,0:T(8,128)S(1)} %bitcast.51), channel_id=1, source_target_pairs={{0,16},{1,17},{2,18},{3,19},{4,20},{5,21},{6,22},{7,23},{8,24},{9,... | collective-permute-start | bytes 12296 | tf_op jit(solution)/shard_map/ppermute | solution.py:53
  34.5 3.6 %collective-permute-start.8 = (bf16[448,1152]{1,0:T(8,128)(2,1)S(1)}, bf16[448,1152]{1,0:T(8,128)(2,1)S(1)}, u32[]{:S(2)}, u32[]{:S(2)}) collective-permute-start(bf16[448,1152]{1,0:T(8,128)(2,1)S(1)} %join.5.refs_0_.refs_8_), channel_id=1, source_target_pairs={{0,1},{1,0},{2,3},{3,2},{4,5},{5,4},{6,7},{7,6},{8,9},{9,8},{10,11... | collective-permute-start | bytes 3096584 | tf_op jit(solution)/shard_map/ppermute | solution.py:53
  46.4 4.3 %collective-permute-start.13 = (bf16[192,1152]{1,0:T(8,128)(2,1)S(1)}, bf16[192,1152]{1,0:T(8,128)(2,1)S(1)}, u32[]{:S(2)}, u32[]{:S(2)}) collective-permute-start(bf16[192,1152]{1,0:T(8,128)(2,1)S(1)} %far_give.1), channel_id=1, source_target_pairs={{0,1},{1,0},{2,3},{3,2},{4,5},{5,4},{6,7},{7,6},{8,9},{9,8},{10,11... | collective-permute-start | bytes 1327112 | tf_op jit(solution)/shard_map/ppermute | solution.py:53
  52.3 2.1 %collective-permute-start.15 = (bf16[192,1152]{1,0:T(8,128)(2,1)S(1)}, bf16[192,1152]{1,0:T(8,128)(2,1)S(1)}, u32[]{:S(2)}, u32[]{:S(2)}) collective-permute-start(bf16[192,1152]{1,0:T(8,128)(2,1)S(1)} %add_convert_fusion), channel_id=1, source_target_pairs={{0,64},{1,193},{2,66},{3,195},{4,68},{5,197},{6,70},{7,199},{8,72}... | collective-permute-start | bytes 1327112 | tf_op jit(solution)/shard_map/ppermute | solution.py:53
  54.4 1.2 %image_sum.5 = bf16[256,1152]{1,0:T(8,128)(2,1)S(1)} custom-call(bf16[256,1152]{1,0:T(8,128)(2,1)S(1)} %collective-permute-done.12.refs_1_.raw_ref, bf16[1024,1152]{1,0:T(8,128)(2,1)S(1)} %normalize.3.yh_ref, bf16[1024,256]{1,0:T(8,128)(2,1)S(1)} %tile.6.refs_3_.g_ref), custom_call_target="tpu_custom_call" | custom-call | flops 276000000 | bytes 1 | tf_op jit(solution)/shard_map/image_sum/pallas_call | solution.py:274
  55.9 1.4 %near_give.1 = bf16[320,1152]{1,0:T(8,128)(2,1)S(1)} custom-call(bf16[1024,256]{1,0:T(8,128)(2,1)S(1)} %tile.4.refs_0_.g_ref, bf16[1024,256]{1,0:T(8,128)(2,1)S(1)} %tile.7.refs_1_.g_ref, bf16[1024,256]{1,0:T(8,128)(2,1)S(1)} %tile.5.refs_2_.g_ref, bf16[1024,256]{1,0:T(8,128)(2,1)S(1)} %tile.6.refs_3_.g_ref, bf16[256,1152]{1,0:T(8,128)(2,1)S(1)} %normalize.4.xh_ref.refs_4_, ...), custom_call_target="tpu_custom_call" | custom-call | flops 240000000 | bytes 1 | tf_op jit(solution)/shard_map/near_give/pallas_call | solution.py:291
  57.7 1.2 %image_sum.7 = bf16[256,1152]{1,0:T(8,128)(2,1)S(1)} custom-call(bf16[256,1152]{1,0:T(8,128)(2,1)S(1)} %collective-permute-done.11.refs_0_.raw_ref, bf16[1024,1152]{1,0:T(8,128)(2,1)S(1)} %normalize.3.yh_ref, bf16[1024,256]{1,0:T(8,128)(2,1)S(1)} %tile.5.refs_2_.g_ref), custom_call_target="tpu_custom_call" | custom-call | flops 276000000 | bytes 1 | tf_op jit(solution)/shard_map/image_sum/pallas_call | solution.py:274
  60.7 2.5 %collective-permute-start.16 = (bf16[256,1152]{1,0:T(8,128)(2,1)S(1)}, bf16[256,1152]{1,0:T(8,128)(2,1)S(1)}, u32[]{:S(2)}, u32[]{:S(2)}) collective-permute-start(bf16[256,1152]{1,0:T(8,128)(2,1)S(1)} %image_sum.6), channel_id=1, source_target_pairs={{0,24},{1,7},{2,26},{3,1},{4,28},{5,3},{6,30},{7,5},{8,0},{9,15},{... | collective-permute-start | bytes 1769480 | tf_op jit(solution)/shard_map/ppermute | solution.py:53
  63.2 1.4 %near_keep.1 = bf16[320,1152]{1,0:T(8,128)(2,1)S(1)} custom-call(bf16[1024,256]{1,0:T(8,128)(2,1)S(1)} %tile.4.refs_0_.g_ref, bf16[1024,256]{1,0:T(8,128)(2,1)S(1)} %tile.7.refs_1_.g_ref, bf16[1024,256]{1,0:T(8,128)(2,1)S(1)} %tile.5.refs_2_.g_ref, bf16[1024,256]{1,0:T(8,128)(2,1)S(1)} %tile.6.refs_3_.g_ref, bf16[256,1152]{1,0:T(8,128)(2,1)S(1)} %normalize.4.xh_ref.refs_4_, ...), custom_call_target="tpu_custom_call" | custom-call | flops 240000000 | bytes 1 | tf_op jit(solution)/shard_map/near_keep/pallas_call | solution.py:291
  64.5 1.2 %image_sum.4 = bf16[256,1152]{1,0:T(8,128)(2,1)S(1)} custom-call(bf16[256,1152]{1,0:T(8,128)(2,1)S(1)} %join.3.refs_0_.raw_ref, bf16[1024,1152]{1,0:T(8,128)(2,1)S(1)} %normalize.3.yh_ref, bf16[1024,256]{1,0:T(8,128)(2,1)S(1)} %tile.4.refs_0_.g_ref), custom_call_target="tpu_custom_call" | custom-call | flops 276000000 | bytes 1 | tf_op jit(solution)/shard_map/image_sum/pallas_call | solution.py:274
  66.1 3.1 %collective-permute-start.23 = (bf16[128,1152]{1,0:T(8,128)(2,1)S(1)}, bf16[128,1152]{1,0:T(8,128)(2,1)S(1)}, u32[]{:S(2)}, u32[]{:S(2)}) collective-permute-start(bf16[128,1152]{1,0:T(8,128)(2,1)S(1)} %pad_maximum_fusion), channel_id=1, source_target_pairs={{0,64},{1,193},{2,66},{3,195},{4,68},{5,197},{6,70},{7,199},{8,72}... | collective-permute-start | bytes 884744 | tf_op jit(solution)/shard_map/ppermute | solution.py:53
  69.3 3.3 %collective-permute-done.17 = bf16[256,1152]{1,0:T(8,128)(2,1)S(1)} collective-permute-done((bf16[256,1152]{1,0:T(8,128)(2,1)S(1)}, bf16[256,1152]{1,0:T(8,128)(2,1)S(1)}, u32[]{:S(2)}, u32[]{:S(2)}) %collective-permute-start.17) | collective-permute-done | bytes 589856 | tf_op jit(solution)/shard_map/ppermute | solution.py:53
  73.2 1.2 %collective-permute-start.20 = (bf16[64,1152]{1,0:T(8,128)(2,1)S(1)}, bf16[64,1152]{1,0:T(8,128)(2,1)S(1)}, u32[]{:S(2)}, u32[]{:S(2)}) collective-permute-start(bf16[64,1152]{1,0:T(8,128)(2,1)S(1)} %get-tuple-element.56), channel_id=1, source_target_pairs={{0,2},{1,9},{2,4},{3,11},{4,6},{5,13},{6,0},{7,15},{8,10},{9,17},{... | collective-permute-start | bytes 442376 | tf_op jit(solution)/shard_map/ppermute | solution.py:53
  74.4 3.2 %collective-permute-done.23.refs_1_ = bf16[128,1152]{1,0:T(8,128)(2,1)S(1)} collective-permute-done((bf16[128,1152]{1,0:T(8,128)(2,1)S(1)}, bf16[128,1152]{1,0:T(8,128)(2,1)S(1)}, u32[]{:S(2)}, u32[]{:S(2)}) %collective-permute-start.23) | collective-permute-done | bytes 294944 | tf_op jit(solution)/shard_map/ppermute | solution.py:53
  77.6 2.6 %collective-permute-done.22.refs_0_ = bf16[128,1152]{1,0:T(8,128)(2,1)S(1)} collective-permute-done((bf16[128,1152]{1,0:T(8,128)(2,1)S(1)}, bf16[128,1152]{1,0:T(8,128)(2,1)S(1)}, u32[]{:S(2)}, u32[]{:S(2)}) %collective-permute-start.22) | collective-permute-done | bytes 294944 | tf_op jit(solution)/shard_map/ppermute | solution.py:53
  80.2 1.8 %collective-permute-start.24 = (bf16[64,1152]{1,0:T(8,128)(2,1)S(1)}, bf16[64,1152]{1,0:T(8,128)(2,1)S(1)}, u32[]{:S(2)}, u32[]{:S(2)}) collective-permute-start(bf16[64,1152]{1,0:T(8,128)(2,1)S(1)} %add_convert_fusion.1), channel_id=1, source_target_pairs={{0,1},{1,0},{2,3},{3,2},{4,5},{5,4},{6,7},{7,6},{8,9},{9,8},{10,11... | collective-permute-start | bytes 442376 | tf_op jit(solution)/shard_map/ppermute | solution.py:53
  (69 shorter events, 21.3 us)
Async XLA Ops:
  0.6 8.4 %collective-permute-start.3 = (bf16[64,1152]{1,0:T(8,128)(2,1)}, bf16[64,1152]{1,0:T(8,128)(2,1)S(1)}, u32[]{:S(2)}, u32[]{:S(2)}) collective-permute-start(bf16[64,1152]{1,0:T(8,128)(2,1)} %refs_1_.1), channel_id=1, source_target_pairs={{0,1},{1,0},{2,3},{3,2},{4,5},{5,4},{6,7},{7,6},{8,9},{9,8},{10,11... | collective-permute-start | bytes 442376 | tf_op jit(solution)/shard_map/ppermute | solution.py:53
  4.0 11.2 %collective-permute-start = (bf16[64,1152]{1,0:T(8,128)(2,1)}, bf16[64,1152]{1,0:T(8,128)(2,1)S(1)}, u32[]{:S(2)}, u32[]{:S(2)}) collective-permute-start(bf16[64,1152]{1,0:T(8,128)(2,1)} %refs_0_.1), channel_id=1, source_target_pairs={{0,2},{1,9},{2,4},{3,11},{4,6},{5,13},{6,0},{7,15},{8,10},{9,17},{... | collective-permute-start | bytes 442376 | tf_op jit(solution)/shard_map/ppermute | solution.py:53
  4.0 11.2 %collective-permute-start.2 = (bf16[64,1152]{1,0:T(8,128)(2,1)}, bf16[64,1152]{1,0:T(8,128)(2,1)S(1)}, u32[]{:S(2)}, u32[]{:S(2)}) collective-permute-start(bf16[64,1152]{1,0:T(8,128)(2,1)} %refs_0_.1), channel_id=1, source_target_pairs={{0,4},{1,17},{2,6},{3,19},{4,0},{5,21},{6,2},{7,23},{8,12},{9,25},... | collective-permute-start | bytes 442376 | tf_op jit(solution)/shard_map/ppermute | solution.py:53
  6.1 9.1 %collective-permute-start.1 = (bf16[64,1152]{1,0:T(8,128)(2,1)}, bf16[64,1152]{1,0:T(8,128)(2,1)S(1)}, u32[]{:S(2)}, u32[]{:S(2)}) collective-permute-start(bf16[64,1152]{1,0:T(8,128)(2,1)} %refs_0_.1), channel_id=1, source_target_pairs={{0,6},{1,25},{2,0},{3,27},{4,2},{5,29},{6,4},{7,31},{8,14},{9,1},{... | collective-permute-start | bytes 442376 | tf_op jit(solution)/shard_map/ppermute | solution.py:53
  9.1 12.9 %collective-permute-start.4 = (bf16[128,1152]{1,0:T(8,128)(2,1)S(1)}, bf16[128,1152]{1,0:T(8,128)(2,1)S(1)}, u32[]{:S(2)}, u32[]{:S(2)}) collective-permute-start(bf16[128,1152]{1,0:T(8,128)(2,1)S(1)} %join.4), channel_id=1, source_target_pairs={{0,64},{1,193},{2,66},{3,195},{4,68},{5,197},{6,70},{7,199},{8,72}... | collective-permute-start | bytes 884744 | tf_op jit(solution)/shard_map/ppermute | solution.py:53
  15.3 22.9 %collective-permute-start.12 = (bf16[256,1152]{1,0:T(8,128)(2,1)S(1)}, bf16[256,1152]{1,0:T(8,128)(2,1)S(1)}, u32[]{:S(2)}, u32[]{:S(2)}) collective-permute-start(bf16[256,1152]{1,0:T(8,128)(2,1)S(1)} %join.3.refs_0_.raw_ref), channel_id=1, source_target_pairs={{0,16},{1,5},{2,18},{3,7},{4,20},{5,1},{6,22},{7,3},{8,24},{9,13},... | collective-permute-start | bytes 1769480 | tf_op jit(solution)/shard_map/ppermute | solution.py:53
  18.1 20.0 %collective-permute-start.11 = (bf16[256,1152]{1,0:T(8,128)(2,1)S(1)}, bf16[256,1152]{1,0:T(8,128)(2,1)S(1)}, u32[]{:S(2)}, u32[]{:S(2)}) collective-permute-start(bf16[256,1152]{1,0:T(8,128)(2,1)S(1)} %join.3.refs_0_.raw_ref), channel_id=1, source_target_pairs={{0,24},{1,7},{2,26},{3,1},{4,28},{5,3},{6,30},{7,5},{8,0},{9,15},{... | collective-permute-start | bytes 1769480 | tf_op jit(solution)/shard_map/ppermute | solution.py:53
  22.0 7.4 %collective-permute-start.5 = (bf16[128,1152]{1,0:T(8,128)(2,1)S(1)}, bf16[128,1152]{1,0:T(8,128)(2,1)S(1)}, u32[]{:S(2)}, u32[]{:S(2)}) collective-permute-start(bf16[128,1152]{1,0:T(8,128)(2,1)S(1)} %collective-permute-done.4.src.refs_3_), channel_id=1, source_target_pairs={{0,32},{1,225},{2,34},{3,227},{4,36},{5,229},{6,38},{7,231},{8,40}... | collective-permute-start | bytes 884744 | tf_op jit(solution)/shard_map/ppermute | solution.py:53
  24.4 7.4 %collective-permute-start.7 = (bf16[128,1152]{1,0:T(8,128)(2,1)S(1)}, bf16[128,1152]{1,0:T(8,128)(2,1)S(1)}, u32[]{:S(2)}, u32[]{:S(2)}) collective-permute-start(bf16[128,1152]{1,0:T(8,128)(2,1)S(1)} %join.4), channel_id=1, source_target_pairs={{0,32},{1,225},{2,34},{3,227},{4,36},{5,229},{6,38},{7,231},{8,40}... | collective-permute-start | bytes 884744 | tf_op jit(solution)/shard_map/ppermute | solution.py:53
  26.6 7.8 %collective-permute-start.6 = (bf16[64,1152]{1,0:T(8,128)(2,1)S(1)}, bf16[64,1152]{1,0:T(8,128)(2,1)S(1)}, u32[]{:S(2)}, u32[]{:S(2)}) collective-permute-start(bf16[64,1152]{1,0:T(8,128)(2,1)S(1)} %head.1), channel_id=1, source_target_pairs={{0,64},{1,193},{2,66},{3,195},{4,68},{5,197},{6,70},{7,199},{8,72}... | collective-permute-start | bytes 442376 | tf_op jit(solution)/shard_map/ppermute | solution.py:53
  29.4 14.8 %collective-permute-start.9 = (bf16[256,1152]{1,0:T(8,128)(2,1)S(1)}, bf16[256,1152]{1,0:T(8,128)(2,1)S(1)}, u32[]{:S(2)}, u32[]{:S(2)}) collective-permute-start(bf16[256,1152]{1,0:T(8,128)(2,1)S(1)} %join.3.refs_0_.raw_ref), channel_id=1, source_target_pairs={{0,8},{1,3},{2,10},{3,5},{4,12},{5,7},{6,14},{7,1},{8,16},{9,11},{... | collective-permute-start | bytes 1769480 | tf_op jit(solution)/shard_map/ppermute | solution.py:53
  31.8 6.7 %collective-permute-start.10 = (s32[8,128]{1,0:T(8,128)S(1)}, s32[8,128]{1,0:T(8,128)S(1)}, u32[]{:S(2)}, u32[]{:S(2)}) collective-permute-start(s32[8,128]{1,0:T(8,128)S(1)} %bitcast.51), channel_id=1, source_target_pairs={{0,16},{1,17},{2,18},{3,19},{4,20},{5,21},{6,22},{7,23},{8,24},{9,... | collective-permute-start | bytes 12296 | tf_op jit(solution)/shard_map/ppermute | solution.py:53
  34.5 5.9 %collective-permute-start.8 = (bf16[448,1152]{1,0:T(8,128)(2,1)S(1)}, bf16[448,1152]{1,0:T(8,128)(2,1)S(1)}, u32[]{:S(2)}, u32[]{:S(2)}) collective-permute-start(bf16[448,1152]{1,0:T(8,128)(2,1)S(1)} %join.5.refs_0_.refs_8_), channel_id=1, source_target_pairs={{0,1},{1,0},{2,3},{3,2},{4,5},{5,4},{6,7},{7,6},{8,9},{9,8},{10,11... | collective-permute-start | bytes 3096584 | tf_op jit(solution)/shard_map/ppermute | solution.py:53
  46.4 5.8 %collective-permute-start.13 = (bf16[192,1152]{1,0:T(8,128)(2,1)S(1)}, bf16[192,1152]{1,0:T(8,128)(2,1)S(1)}, u32[]{:S(2)}, u32[]{:S(2)}) collective-permute-start(bf16[192,1152]{1,0:T(8,128)(2,1)S(1)} %far_give.1), channel_id=1, source_target_pairs={{0,1},{1,0},{2,3},{3,2},{4,5},{5,4},{6,7},{7,6},{8,9},{9,8},{10,11... | collective-permute-start | bytes 1327112 | tf_op jit(solution)/shard_map/ppermute | solution.py:53
  52.3 13.4 %collective-permute-start.15 = (bf16[192,1152]{1,0:T(8,128)(2,1)S(1)}, bf16[192,1152]{1,0:T(8,128)(2,1)S(1)}, u32[]{:S(2)}, u32[]{:S(2)}) collective-permute-start(bf16[192,1152]{1,0:T(8,128)(2,1)S(1)} %add_convert_fusion), channel_id=1, source_target_pairs={{0,64},{1,193},{2,66},{3,195},{4,68},{5,197},{6,70},{7,199},{8,72}... | collective-permute-start | bytes 1327112 | tf_op jit(solution)/shard_map/ppermute | solution.py:53
  55.6 16.9 %collective-permute-start.18 = (bf16[256,1152]{1,0:T(8,128)(2,1)S(1)}, bf16[256,1152]{1,0:T(8,128)(2,1)S(1)}, u32[]{:S(2)}, u32[]{:S(2)}) collective-permute-start(bf16[256,1152]{1,0:T(8,128)(2,1)S(1)} %image_sum.5), channel_id=1, source_target_pairs={{0,16},{1,5},{2,18},{3,7},{4,20},{5,1},{6,22},{7,3},{8,24},{9,13},... | collective-permute-start | bytes 1769480 | tf_op jit(solution)/shard_map/ppermute | solution.py:53
  57.3 8.5 %collective-permute-start.14 = (bf16[320,1152]{1,0:T(8,128)(2,1)S(1)}, bf16[320,1152]{1,0:T(8,128)(2,1)S(1)}, u32[]{:S(2)}, u32[]{:S(2)}) collective-permute-start(bf16[320,1152]{1,0:T(8,128)(2,1)S(1)} %near_give.1), channel_id=1, source_target_pairs={{0,1},{1,0},{2,3},{3,2},{4,5},{5,4},{6,7},{7,6},{8,9},{9,8},{10,11... | collective-permute-start | bytes 2211848 | tf_op jit(solution)/shard_map/ppermute | solution.py:53
  58.9 13.6 %collective-permute-start.17 = (bf16[256,1152]{1,0:T(8,128)(2,1)S(1)}, bf16[256,1152]{1,0:T(8,128)(2,1)S(1)}, u32[]{:S(2)}, u32[]{:S(2)}) collective-permute-start(bf16[256,1152]{1,0:T(8,128)(2,1)S(1)} %image_sum.7), channel_id=1, source_target_pairs={{0,8},{1,3},{2,10},{3,5},{4,12},{5,7},{6,14},{7,1},{8,16},{9,11},{... | collective-permute-start | bytes 1769480 | tf_op jit(solution)/shard_map/ppermute | solution.py:53
  60.7 11.8 %collective-permute-start.16 = (bf16[256,1152]{1,0:T(8,128)(2,1)S(1)}, bf16[256,1152]{1,0:T(8,128)(2,1)S(1)}, u32[]{:S(2)}, u32[]{:S(2)}) collective-permute-start(bf16[256,1152]{1,0:T(8,128)(2,1)S(1)} %image_sum.6), channel_id=1, source_target_pairs={{0,24},{1,7},{2,26},{3,1},{4,28},{5,3},{6,30},{7,5},{8,0},{9,15},{... | collective-permute-start | bytes 1769480 | tf_op jit(solution)/shard_map/ppermute | solution.py:53
  66.1 11.4 %collective-permute-start.23 = (bf16[128,1152]{1,0:T(8,128)(2,1)S(1)}, bf16[128,1152]{1,0:T(8,128)(2,1)S(1)}, u32[]{:S(2)}, u32[]{:S(2)}) collective-permute-start(bf16[128,1152]{1,0:T(8,128)(2,1)S(1)} %pad_maximum_fusion), channel_id=1, source_target_pairs={{0,64},{1,193},{2,66},{3,195},{4,68},{5,197},{6,70},{7,199},{8,72}... | collective-permute-start | bytes 884744 | tf_op jit(solution)/shard_map/ppermute | solution.py:53
  69.3 10.9 %collective-permute-start.22 = (bf16[128,1152]{1,0:T(8,128)(2,1)S(1)}, bf16[128,1152]{1,0:T(8,128)(2,1)S(1)}, u32[]{:S(2)}, u32[]{:S(2)}) collective-permute-start(bf16[128,1152]{1,0:T(8,128)(2,1)S(1)} %slice.46), channel_id=1, source_target_pairs={{0,32},{1,225},{2,34},{3,227},{4,36},{5,229},{6,38},{7,231},{8,40}... | collective-permute-start | bytes 884744 | tf_op jit(solution)/shard_map/ppermute | solution.py:53
  72.9 9.1 %collective-permute-start.19 = (bf16[64,1152]{1,0:T(8,128)(2,1)S(1)}, bf16[64,1152]{1,0:T(8,128)(2,1)S(1)}, u32[]{:S(2)}, u32[]{:S(2)}) collective-permute-start(bf16[64,1152]{1,0:T(8,128)(2,1)S(1)} %get-tuple-element.54), channel_id=1, source_target_pairs={{0,6},{1,25},{2,0},{3,27},{4,2},{5,29},{6,4},{7,31},{8,14},{9,1},{... | collective-permute-start | bytes 442376 | tf_op jit(solution)/shard_map/ppermute | solution.py:53
  73.0 9.1 %collective-permute-start.21 = (bf16[64,1152]{1,0:T(8,128)(2,1)S(1)}, bf16[64,1152]{1,0:T(8,128)(2,1)S(1)}, u32[]{:S(2)}, u32[]{:S(2)}) collective-permute-start(bf16[64,1152]{1,0:T(8,128)(2,1)S(1)} %get-tuple-element.55), channel_id=1, source_target_pairs={{0,4},{1,17},{2,6},{3,19},{4,0},{5,21},{6,2},{7,23},{8,12},{9,25},... | collective-permute-start | bytes 442376 | tf_op jit(solution)/shard_map/ppermute | solution.py:53
  73.2 8.8 %collective-permute-start.20 = (bf16[64,1152]{1,0:T(8,128)(2,1)S(1)}, bf16[64,1152]{1,0:T(8,128)(2,1)S(1)}, u32[]{:S(2)}, u32[]{:S(2)}) collective-permute-start(bf16[64,1152]{1,0:T(8,128)(2,1)S(1)} %get-tuple-element.56), channel_id=1, source_target_pairs={{0,2},{1,9},{2,4},{3,11},{4,6},{5,13},{6,0},{7,15},{8,10},{9,17},{... | collective-permute-start | bytes 442376 | tf_op jit(solution)/shard_map/ppermute | solution.py:53
  (4 other events, 9.1 us)
